TPU v7x, 128 devices: a whole 4x4x4 slice. The times are simulated.
128 devices in a mesh: outer: 16 (over z_lo, y, core), blk: 8 (over x, z_hi).
Axes of the slice: x: 4, y: 4, z: 4 (z_hi: 2, z_lo: 2; z = z_hi * 2 + z_lo), core: 2. Of those that a mesh axis runs over, the one named last changes fastest.
Arguments:
- images: bfloat16 [20480, 1152], P(('outer', 'blk')), may hold values from -0.1796875 to 0.1796875
- texts: bfloat16 [20480, 1152], P(('outer', 'blk')), may hold values from -0.1796875 to 0.1796875
- temp: float32 [1], replicated, may hold values from 2 to 12
- bias: float32 [1], replicated, may hold values from -4 to -1
Outputs:
- grad_images: bfloat16 [20480, 1152], P(('outer', 'blk'))
- grad_texts: bfloat16 [20480, 1152], P(('outer', 'blk'))
All inputs are finite; a program needn't handle non-finite values.
Results may differ from a plain program's by a relative error of at most 0.018.
Values may be sent and summed in bfloat16 or wider, within the bound.
No kernel may reach another device: no remote copies, remote signals or barrier semaphores. Data moves between devices by JAX's collectives and lax.ppermute only.
A program may use at most 128 MiB of HBM per device.

v0:
```python
import jax
import jax.numpy as jnp
from jax import lax
from jax.sharding import PartitionSpec as P


def shifted(value, axis, steps):
    count = lax.axis_size(axis)
    pairs = [(source, (source + steps) % count) for source in range(count)]
    return lax.ppermute(value, axis, pairs)


def normalize(rows):
    values = rows.astype(jnp.float32)
    length = jnp.sqrt(jnp.sum(values * values, axis=-1, keepdims=True) + 1e-06)
    return (values / length, length)


def pair_scores(left, right):
    return lax.dot_general(
        left, right, (((1,), (1,)), ((), ())), preferred_element_type=jnp.float32
    )


def left_product(weights, right):
    return lax.dot_general(
        weights, right, (((0,), (0,)), ((), ())), preferred_element_type=jnp.float32
    )


def local(images, texts, temp, bias):
    scale = temp[0]
    offset = bias[0]
    rows = images.shape[0]
    width = images.shape[1]
    first = lax.axis_index("blk") * rows
    ximg, img_len = normalize(images)
    xtxt, txt_len = normalize(texts)
    img_n = ximg.astype(jnp.bfloat16)
    txt_n = xtxt.astype(jnp.bfloat16)
    txt_prev = shifted(txt_n, "outer", 1)

    def signal(left, right, match):
        logit = scale * pair_scores(left, right) + offset
        return (jax.nn.sigmoid(logit) - match).astype(jnp.bfloat16)

    own_piece = lax.all_gather(txt_n, "blk", axis=0, tiled=True)
    prev_piece = lax.all_gather(txt_prev, "blk", axis=0, tiled=True)
    count = own_piece.shape[0]
    image_ids = first + lax.broadcasted_iota(jnp.int32, (rows, count), 0)
    text_ids = lax.broadcasted_iota(jnp.int32, (rows, count), 1)
    sig_own = signal(img_n, own_piece, (image_ids == text_ids).astype(jnp.float32))
    sig_prev = signal(img_n, prev_piece, 0.0)
    total = jnp.dot(sig_own, own_piece, preferred_element_type=jnp.float32)
    total = total + jnp.dot(sig_prev, prev_piece, preferred_element_type=jnp.float32)
    folded = (total, sig_own, sig_prev)
    img_total, sig_own_all, extra_all = folded
    summed = lax.psum_scatter(
        (
            scale
            * jnp.concatenate(
                [left_product(sig_own_all, img_n), left_product(extra_all, img_n)], axis=1
            )
        ).astype(jnp.bfloat16),
        "blk",
        scatter_dimension=0,
        tiled=True,
    ).astype(jnp.float32)
    txt_own = summed[:, :width]
    txt_back = summed[:, width:]
    dimg = scale * img_total
    returned = shifted(txt_back.astype(jnp.bfloat16), "outer", -1).astype(txt_back.dtype)
    dtxt = txt_own + returned
    grad_images = (dimg - ximg * jnp.sum(ximg * dimg, axis=-1, keepdims=True)) / img_len
    grad_texts = (dtxt - xtxt * jnp.sum(xtxt * dtxt, axis=-1, keepdims=True)) / txt_len
    return (grad_images.astype(jnp.bfloat16), grad_texts.astype(jnp.bfloat16))


def solution(mesh):
    return jax.shard_map(
        local,
        mesh=mesh,
        in_specs=(P(("outer", "blk"), None), P(("outer", "blk"), None), P(), P()),
        out_specs=(P(("outer", "blk"), None), P(("outer", "blk"), None)),
        check_vma=False,
    )
```

profile of v0, /device:TPU:0, one launch (start us, length us, event | category | flops | bytes accessed | tf_op | source)
XLA Modules:
  0.0 273.7 jit_solution(5741619802566617859)
XLA Ops:
  7.2 1.1 fusion.16
  8.4 1.9 fusion.18
  10.4 0.1 collective-permute-start
  10.4 9.3 %collective-permute-done = bf16[160,1152]{1,0:T(8,128)(2,1)S(1)} collective-permute-done((bf16[160,1152]{1,0:T(8,128)(2,1)}, bf16[160,1152]{1,0:T(8,128)(2,1)S(1)}, u32[]{:S(2)}, u32[]{:S(2)}) %collective-permute-start) | collective-permute-done | bytes 368672 | tf_op jit(solution)/shard_map/ppermute | solution.py:10
  19.7 0.7 copy-done.2
  20.5 0.0 reduce-scatter.4.cloned.1.call-start
  21.8 1.2 fusion.15
  23.0 51.8 %all-gather.3.cloned.1.call-done = bf16[1280,1152]{1,0:T(8,128)(2,1)} async-done(((bf16[160,1152]{1,0:T(8,128)(2,1)}), bf16[1280,1152]{1,0:T(8,128)(2,1)}) %all-gather.3.cloned.1.call-update) | async-done | bytes 2949136 | tf_op jit(solution)/shard_map/all_gather | solution.py:47
  74.9 3.0 %fusion.13 = bf16[160,1280]{1,0:T(8,128)(2,1)S(1)} fusion(bf16[1280,1152]{1,0:T(8,128)(2,1)} %all-gather.3.cloned.1.call-done, s32[160]{0:T(256)S(1)} %iota_add_fusion, f32[]{:T(128)} %bitcast.15, f32[]{:T(128)} %bitcast.12, f32[160]{0:T(256)S(1)} %add_sqrt_fusion.1, bf16[160,1152]{1,0:T(8,128)(2,1)} %param.4), kind=kOutput, calls=%fused_computation.17 | convolution fusion | flops 474255360 | bytes 3728648 | tf_op jit(solution)/shard_map/dot_general | solution.py:20
  77.9 3.6 %fusion.21 = f32[1280,1152]{0,1:T(8,128)} fusion(bf16[160,1280]{1,0:T(8,128)(2,1)S(1)} %fusion.13, f32[160]{0:T(256)S(1)} %add_sqrt_fusion.1, bf16[160,1152]{1,0:T(8,128)(2,1)S(1)} %copy-done.1), kind=kOutput, calls=%fused_computation.37 | convolution fusion | flops 472412160 | bytes 6677120 | tf_op jit(solution)/shard_map/dot_general | solution.py:26
  81.5 56.2 %all-gather.5.cloned.1.call-done = bf16[1280,1152]{1,0:T(8,128)(2,1)} async-done(((bf16[160,1152]{1,0:T(8,128)(2,1)}), bf16[1280,1152]{1,0:T(8,128)(2,1)}) %all-gather.5.cloned.1.call-update) | async-done | bytes 2949136 | tf_op jit(solution)/shard_map/all_gather | solution.py:48
  137.7 2.9 %fusion.14 = bf16[160,1280]{1,0:T(8,128)(2,1)S(1)} fusion(bf16[1280,1152]{1,0:T(8,128)(2,1)} %all-gather.5.cloned.1.call-done, f32[]{:T(128)} %bitcast.16, f32[]{:T(128)} %bitcast.14, f32[160]{0:T(256)S(1)} %add_sqrt_fusion.1, bf16[160,1152]{1,0:T(8,128)(2,1)S(1)} %copy-done.1), kind=kOutput, calls=%fused_computation.18 | convolution fusion | flops 473640960 | bytes 3728008 | tf_op jit(solution)/shard_map/dot_general | solution.py:20
  140.6 3.6 %fusion.19 = f32[1280,1152]{0,1:T(8,128)} fusion(bf16[160,1280]{1,0:T(8,128)(2,1)S(1)} %fusion.14, f32[160]{0:T(256)S(1)} %add_sqrt_fusion.1, bf16[160,1152]{1,0:T(8,128)(2,1)S(1)} %copy-done.1), kind=kOutput, calls=%fused_computation.36 | convolution fusion | flops 472412160 | bytes 6677120 | tf_op jit(solution)/shard_map/dot_general | solution.py:26
  144.3 7.9 %fusion = bf16[1280,2304]{0,1:T(8,128)(2,1)} fusion(f32[1280,1152]{0,1:T(8,128)} %fusion.19, f32[1280,1152]{0,1:T(8,128)} %fusion.21, f32[]{:T(128)} %bitcast.13), kind=kLoop, calls=%fused_computation.1 | loop fusion | flops 8847360 | bytes 17694724 | tf_op jit(solution)/shard_map/convert_element_type | solution.py:64
  152.2 8.8 %copy.10 = bf16[1280,2304]{1,0:T(8,128)(2,1)} copy(bf16[1280,2304]{0,1:T(8,128)(2,1)} %fusion) | data formatting | bytes 11796480
  161.0 2.6 fusion.25
  163.6 2.7 multiply_reduce_fusion.1
  166.3 89.8 %reduce-scatter.4.cloned.1.call-done = bf16[160,2304]{1,0:T(8,128)(2,1)} async-done(((bf16[1280,2304]{1,0:T(8,128)(2,1)}), bf16[160,2304]{1,0:T(8,128)(2,1)}) %reduce-scatter.4.cloned.1.call-update) | async-done | bytes 737296 | tf_op jit(solution)/shard_map/reduce_scatter | solution.py:58
  256.1 1.0 slice.14
  257.1 1.7 collective-permute-start.1
  258.8 1.0 divide_convert_fusion.1
  259.8 4.1 %collective-permute-done.1 = bf16[160,1152]{1,0:T(8,128)(2,1)S(1)} collective-permute-done((bf16[160,1152]{1,0:T(8,128)(2,1)S(1)}, bf16[160,1152]{1,0:T(8,128)(2,1)S(1)}, u32[]{:S(2)}, u32[]{:S(2)}) %collective-permute-start.1) | collective-permute-done | bytes 368672 | tf_op jit(solution)/shard_map/ppermute | solution.py:10
  263.9 1.3 multiply_reduce_fusion
  265.2 2.0 divide_convert_fusion
  (13 shorter events, 0.2 us)
Async XLA Ops:
  7.2 67.7 %all-gather.3.cloned.1.call-start = ((), (), s32[]{:S(2)}) async-start(), calls=%async_computation.1 | async-start | bytes 3317760 | tf_op jit(solution)/shard_map/all_gather | solution.py:47
  8.4 69.5 %copy-start.1 = (bf16[160,1152]{1,0:T(8,128)(2,1)S(1)}, bf16[160,1152]{1,0:T(8,128)(2,1)}, u32[]{:S(2)}) copy-start(bf16[160,1152]{1,0:T(8,128)(2,1)} %param.4) | copy-start | bytes 1105924
  10.3 127.4 %all-gather.5.cloned.1.call-start = ((), (), s32[]{:S(2)}) async-start(), calls=%async_computation.2 | async-start | bytes 3317760 | tf_op jit(solution)/shard_map/all_gather | solution.py:48
  10.4 9.4 %collective-permute-start = (bf16[160,1152]{1,0:T(8,128)(2,1)}, bf16[160,1152]{1,0:T(8,128)(2,1)S(1)}, u32[]{:S(2)}, u32[]{:S(2)}) collective-permute-start(bf16[160,1152]{1,0:T(8,128)(2,1)} %fusion.18), channel_id=1, source_target_pairs={{0,8},{8,16},{16,24},{24,32},{32,40},{40,48},{48,56},{56,64},{64,7... | collective-permute-start | bytes 1105928 | tf_op jit(solution)/shard_map/ppermute | solution.py:10
  19.7 0.7 copy-start.2
  20.5 235.6 %reduce-scatter.4.cloned.1.call-start = ((), (), s32[]{:S(2)}) async-start(), calls=%async_computation.3 | async-start | bytes 6635520 | tf_op jit(solution)/shard_map/reduce_scatter | solution.py:58
  161.0 102.9 %copy-start = (bf16[160,1152]{1,0:T(8,128)(2,1)S(1)}, bf16[160,1152]{1,0:T(8,128)(2,1)}, u32[]{:S(2)}) copy-start(bf16[160,1152]{1,0:T(8,128)(2,1)} %param.5) | copy-start | bytes 1105924
  257.1 6.8 %collective-permute-start.1 = (bf16[160,1152]{1,0:T(8,128)(2,1)S(1)}, bf16[160,1152]{1,0:T(8,128)(2,1)S(1)}, u32[]{:S(2)}, u32[]{:S(2)}) collective-permute-start(bf16[160,1152]{1,0:T(8,128)(2,1)S(1)} %slice.14), channel_id=1, source_target_pairs={{0,120},{8,0},{16,8},{24,16},{32,24},{40,32},{48,40},{56,48},{64,5... | collective-permute-start | bytes 1105928 | tf_op jit(solution)/shard_map/ppermute | solution.py:10
Sparse Core Ops, SparseCore 0:
  10.9 63.9 all-gather.2
  77.7 59.9 all-gather.4
  161.1 94.8 reduce-scatter.3
where the time goes:
time: 276 us; the launch traced here: 274 us
  waiting for transfers between devices  211 us (76%)
  matrix products  18.5 us (7%)
  other arithmetic  16.4 us (6%)
  between operations  15.1 us (5%)
  local copies, waits for them, and re-layouts  10.6 us (4%)
    reduce_scatter x1, waiting for transfers between devices, local(): lax.psum_scatter((scale * jnp.concatenate([left_product(sig_own_all, img_...  89.8 us
    all_gather x1, waiting for transfers between devices, local(): prev_piece = lax.all_gather(txt_prev, 'blk', axis=0, tiled=True)  56.2 us
    all_gather x1, waiting for transfers between devices, local(): own_piece = lax.all_gather(txt_n, 'blk', axis=0, tiled=True)  51.8 us
    ppermute x2, waiting for transfers between devices, shifted(): return lax.ppermute(value, axis, pairs)  13.3 us
    unnamed x7, local copies, waits for them, and re-layouts  9.56 us
    convert_element_type x1, other arithmetic, local(): summed = lax.psum_scatter((scale * jnp.concatenate([left_product(sig_own_...  7.91 us
    dot_general x2, matrix products, left_product(): lax.dot_general(weights, right, (((0,), (0,)), ((), ())), preferred_eleme...  7.28 us
    dot_general x2, matrix products, pair_scores(): lax.dot_general(left, right, (((1,), (1,)), ((), ())), preferred_element_...  5.91 us
  transfers between devices with their start and end apart: 5, of which 5 were waited for; matrix products, arithmetic and copies ran while one was open for 5% of the time, Pallas kernels for 0%

commit v1 on v0

v1 whole, which is shorter than its diff:
```python
import functools

import jax
import jax.numpy as jnp
from jax import lax
from jax.experimental import pallas as pl
from jax.experimental.pallas import tpu as pltpu
from jax.sharding import PartitionSpec as P

VMEM = pltpu.VMEM
LIMIT = 48 * 1024 * 1024
BLK_X = 4
BLK_Z = 2


def shift_prev(value, steps):
    count = lax.axis_size("outer")
    return lax.ppermute(value, "outer", [(s, (s + steps) % count) for s in range(count)])


def shift_x(value, steps):
    pairs = [
        (x * BLK_Z + z, (x + steps) % BLK_X * BLK_Z + z)
        for x in range(BLK_X)
        for z in range(BLK_Z)
    ]
    return lax.ppermute(value, "blk", pairs)


def swap_z(value):
    pairs = [
        (x * BLK_Z + z, x * BLK_Z + (BLK_Z - 1 - z))
        for x in range(BLK_X)
        for z in range(BLK_Z)
    ]
    return lax.ppermute(value, "blk", pairs)


def normalized(ref):
    values = ref[...].astype(jnp.float32)
    length = jnp.sqrt(jnp.sum(values * values, axis=-1, keepdims=True) + 1e-06)
    return (values / length).astype(jnp.bfloat16)


def pairs_kernel(
    temp, bias, x0, x1, x2, x3, t0, t1, p0, p1,
    own_img, img1, img2, img3, own_txt, part_txt, prev_own, prev_part,
    txt, img, sig,
):
    rows = x0.shape[0]
    scale, offset = temp[0], bias[0]
    for place, ref in enumerate((t0, t1, p0, p1)):
        txt[place * rows : (place + 1) * rows, :] = normalized(ref)
    for place, (ref, out) in enumerate(
        ((x0, own_img), (x1, img1), (x2, img2), (x3, img3))
    ):
        mine = slice(place * rows, (place + 1) * rows)
        unit = normalized(ref)
        img[mine, :] = unit
        scores = lax.dot_general(
            unit, txt[...], (((1,), (1,)), ((), ())), preferred_element_type=jnp.float32
        )
        weight = jax.nn.sigmoid(scale * scores + offset)
        if place == 0:
            row = lax.broadcasted_iota(jnp.int32, weight.shape, 0)
            col = lax.broadcasted_iota(jnp.int32, weight.shape, 1)
            weight = weight - (row == col).astype(jnp.float32)
        weight = weight.astype(jnp.bfloat16)
        sig[mine, :] = weight
        total = jnp.dot(weight, txt[...], preferred_element_type=jnp.float32)
        out[...] = (scale * total).astype(out.dtype)
    for place, out in enumerate((own_txt, part_txt, prev_own, prev_part)):
        mine = slice(place * rows, (place + 1) * rows)
        total = lax.dot_general(
            sig[:, mine], img[...], (((0,), (0,)), ((), ())),
            preferred_element_type=jnp.float32,
        )
        out[...] = (scale * total).astype(out.dtype)


def finish_kernel(raw, own, *rest):
    out = rest[-1]
    values = raw[...].astype(jnp.float32)
    length = jnp.sqrt(jnp.sum(values * values, axis=-1, keepdims=True) + 1e-06)
    unit = values / length
    total = own[...]
    for ref in rest[:-1]:
        total = total + ref[...].astype(jnp.float32)
    inner = jnp.sum(unit * total, axis=-1, keepdims=True)
    out[...] = ((total - unit * inner) / length).astype(out.dtype)


def finish(raw, own, *received):
    return pl.pallas_call(
        finish_kernel,
        out_shape=jax.ShapeDtypeStruct(raw.shape, jnp.bfloat16),
        in_specs=[pl.BlockSpec(memory_space=VMEM)] * (2 + len(received)),
        out_specs=pl.BlockSpec(memory_space=VMEM),
        compiler_params=pltpu.CompilerParams(vmem_limit_bytes=LIMIT),
        name="finish",
    )(raw, own, *received)


def local(images, texts, temp, bias):
    shape = images.shape
    rows, width = shape
    txt_part = swap_z(texts)
    img_1 = shift_x(images, 1)
    img_3 = shift_x(images, -1)
    img_2 = shift_x(images, 2)
    prev_own = shift_prev(texts, 1)
    prev_part = shift_prev(txt_part, 1)

    wide = jax.ShapeDtypeStruct(shape, jnp.float32)
    sent = jax.ShapeDtypeStruct(shape, jnp.bfloat16)
    smem = pl.BlockSpec(memory_space=pltpu.SMEM)
    vmem = pl.BlockSpec(memory_space=VMEM)
    d0, d1, d2, d3, e_own, e_part, f_own, f_part = pl.pallas_call(
        pairs_kernel,
        out_shape=[wide, sent, sent, sent, wide, wide, sent, sent],
        in_specs=[smem] * 2 + [vmem] * 8,
        out_specs=[vmem] * 8,
        scratch_shapes=[
            VMEM((4 * rows, width), jnp.bfloat16),
            VMEM((4 * rows, width), jnp.bfloat16),
            VMEM((4 * rows, 4 * rows), jnp.bfloat16),
        ],
        compiler_params=pltpu.CompilerParams(vmem_limit_bytes=LIMIT),
        name="pairs",
    )(temp, bias, images, img_1, img_2, img_3, texts, txt_part, prev_own, prev_part)

    back_part = shift_prev(f_part, -1)
    r1 = shift_x(d1, -1)
    r3 = shift_x(d3, 1)
    r2 = shift_x(d2, 2)
    back_own = shift_prev(f_own, -1)
    to_part = (e_part + back_part.astype(jnp.float32)).astype(jnp.bfloat16)
    from_part = swap_z(to_part)
    grad_images = finish(images, d0, r1, r2, r3)
    grad_texts = finish(texts, e_own, back_own, from_part)
    return (grad_images, grad_texts)


def solution(mesh):
    spec = P(("outer", "blk"), None)
    return jax.shard_map(
        local,
        mesh=mesh,
        in_specs=(spec, spec, P(), P()),
        out_specs=(spec, spec),
        check_vma=False,
    )
```

time: 276 us -> 61.1 us (0.22)
  waiting for transfers between devices: 211 us -> 32.7 us
  matrix products: 18.5 us -> 0 us
  other arithmetic: 16.4 us -> 1.18 us
  between operations: 15.1 us -> 1.96 us
  starting transfers between devices: 1.94 us -> 13.5 us
  local copies, waits for them, and re-layouts: 10.6 us -> 2.02 us
  Pallas kernels: 0 us -> 8.52 us
    all_gather x2 -> x0, waiting for transfers between devices: 108 us -> none  [the longest x1 56.2 us: local(): prev_piece = lax.all_gather(txt_prev, 'blk', axis=0, tiled=True)]
    reduce_scatter x1 -> x0, waiting for transfers between devices: 89.8 us -> none  [local(): lax.psum_scatter((scale * jnp.concatenate([left_product(sig_own_all, img_...]
    ppermute x2 -> x12, waiting for transfers between devices: 13.3 us -> 32.7 us  [the longest x6 21.6 us: shift_x(): return lax.ppermute(value, 'blk', pairs)]
    dot_general x6 -> x0, matrix products: 18.5 us -> none  [the longest x2 7.28 us: left_product(): lax.dot_general(weights, right, (((0,), (0,)), ((), ())), preferred_eleme...]
    ppermute x2 -> x12, starting transfers between devices: 1.81 us -> 13.5 us  [the longest x6 6.67 us: shift_x(): return lax.ppermute(value, 'blk', pairs)]
    convert_element_type x4 -> x1, other arithmetic: 12.8 us -> 1.18 us  [local(): to_part = (e_part + back_part.astype(jnp.float32)).astype(jnp.bfloat16)]
    pallas_call x0 -> x3, Pallas kernels: none -> 8.52 us  [the longest x1 6.23 us: local(): pl.pallas_call(pairs_kernel, out_shape=[wide, sent, sent, sent, wide, wid...]
    unnamed x7 -> x8, local copies, waits for them, and re-layouts: 9.56 us -> 2.02 us
  transfers between devices with their start and end apart: 5 -> 12, of which waited for: 5 -> 7; matrix products, arithmetic and copies ran while one was open for 5% -> 2% of each run, Pallas kernels for 0% -> 2%
where the time goes in v1:
time: 61.1 us; the launch traced here: 59.9 us
  waiting for transfers between devices  32.7 us (54%)
  starting transfers between devices  13.5 us (22%)
  Pallas kernels  8.52 us (14%)
  local copies, waits for them, and re-layouts  2.02 us (3%)
  between operations  1.96 us (3%)
  other arithmetic  1.18 us (2%)
    ppermute x6, waiting for transfers between devices, shift_x(): return lax.ppermute(value, 'blk', pairs)  21.6 us
    ppermute x2, waiting for transfers between devices, swap_z(): return lax.ppermute(value, 'blk', pairs)  8.3 us
    ppermute x6, starting transfers between devices, shift_x(): return lax.ppermute(value, 'blk', pairs)  6.67 us
    pallas_call x1, Pallas kernels, local(): pl.pallas_call(pairs_kernel, out_shape=[wide, sent, sent, sent, wide, wid...  6.23 us
    ppermute x2, starting transfers between devices, swap_z(): return lax.ppermute(value, 'blk', pairs)  4.18 us
    ppermute x4, waiting for transfers between devices, shift_prev(): lax.ppermute(value, 'outer', [(s, (s + steps) % count) for s in range(cou...  2.81 us
    ppermute x4, starting transfers between devices, shift_prev(): lax.ppermute(value, 'outer', [(s, (s + steps) % count) for s in range(cou...  2.66 us
    pallas_call x2, Pallas kernels, finish(): pl.pallas_call(finish_kernel, out_shape=jax.ShapeDtypeStruct(raw.shape, j...  2.29 us
  transfers between devices with their start and end apart: 12, of which 7 were waited for; matrix products, arithmetic and copies ran while one was open for 2% of the time, Pallas kernels for 2%

profile of v1, /device:TPU:0, one launch (start us, length us, event | category | flops | bytes accessed | tf_op | source)
XLA Modules:
  0.0 59.9 jit_solution(6070097508033185867)
XLA Ops:
  0.6 4.0 %collective-permute-start.3 = (bf16[160,1152]{1,0:T(8,128)(2,1)}, bf16[160,1152]{1,0:T(8,128)(2,1)S(1)}, u32[]{:S(2)}, u32[]{:S(2)}) collective-permute-start(bf16[160,1152]{1,0:T(8,128)(2,1)} %raw.3), channel_id=1, source_target_pairs={{0,1},{1,0},{2,3},{3,2},{4,5},{5,4},{6,7},{7,6},{8,9},{9,8},{10,11... | collective-permute-start | bytes 1105928 | tf_op jit(solution)/shard_map/ppermute | solution.py:36
  4.7 0.0 collective-permute-start.4
  4.7 2.8 %collective-permute-start.2 = (bf16[160,1152]{1,0:T(8,128)(2,1)}, bf16[160,1152]{1,0:T(8,128)(2,1)S(1)}, u32[]{:S(2)}, u32[]{:S(2)}) collective-permute-start(bf16[160,1152]{1,0:T(8,128)(2,1)} %raw.2), channel_id=1, source_target_pairs={{0,6},{1,7},{2,0},{3,1},{4,2},{5,3},{6,4},{7,5},{8,14},{9,15},{10,... | collective-permute-start | bytes 1105928 | tf_op jit(solution)/shard_map/ppermute | solution.py:27
  7.4 0.8 %collective-permute-start.1 = (bf16[160,1152]{1,0:T(8,128)(2,1)}, bf16[160,1152]{1,0:T(8,128)(2,1)S(1)}, u32[]{:S(2)}, u32[]{:S(2)}) collective-permute-start(bf16[160,1152]{1,0:T(8,128)(2,1)} %raw.2), channel_id=1, source_target_pairs={{0,4},{1,5},{2,6},{3,7},{4,0},{5,1},{6,2},{7,3},{8,12},{9,13},{10,... | collective-permute-start | bytes 1105928 | tf_op jit(solution)/shard_map/ppermute | solution.py:27
  8.2 0.9 %collective-permute-start = (bf16[160,1152]{1,0:T(8,128)(2,1)}, bf16[160,1152]{1,0:T(8,128)(2,1)S(1)}, u32[]{:S(2)}, u32[]{:S(2)}) collective-permute-start(bf16[160,1152]{1,0:T(8,128)(2,1)} %raw.2), channel_id=1, source_target_pairs={{0,2},{1,3},{2,4},{3,5},{4,6},{5,7},{6,0},{7,1},{8,10},{9,11},{10,... | collective-permute-start | bytes 1105928 | tf_op jit(solution)/shard_map/ppermute | solution.py:27
  9.1 8.3 %collective-permute-done.3.t1 = bf16[160,1152]{1,0:T(8,128)(2,1)S(1)} collective-permute-done((bf16[160,1152]{1,0:T(8,128)(2,1)}, bf16[160,1152]{1,0:T(8,128)(2,1)S(1)}, u32[]{:S(2)}, u32[]{:S(2)}) %collective-permute-start.3) | collective-permute-done | bytes 368672 | tf_op jit(solution)/shard_map/ppermute | solution.py:36
  18.7 5.1 %collective-permute-done.2.x3 = bf16[160,1152]{1,0:T(8,128)(2,1)S(1)} collective-permute-done((bf16[160,1152]{1,0:T(8,128)(2,1)}, bf16[160,1152]{1,0:T(8,128)(2,1)S(1)}, u32[]{:S(2)}, u32[]{:S(2)}) %collective-permute-start.2) | collective-permute-done | bytes 368672 | tf_op jit(solution)/shard_map/ppermute | solution.py:27
  23.8 4.7 %collective-permute-done.x1 = bf16[160,1152]{1,0:T(8,128)(2,1)S(1)} collective-permute-done((bf16[160,1152]{1,0:T(8,128)(2,1)}, bf16[160,1152]{1,0:T(8,128)(2,1)S(1)}, u32[]{:S(2)}, u32[]{:S(2)}) %collective-permute-start) | collective-permute-done | bytes 368672 | tf_op jit(solution)/shard_map/ppermute | solution.py:27
  28.5 1.0 %copy-done = bf16[160,1152]{1,0:T(8,128)(2,1)S(1)} copy-done((bf16[160,1152]{1,0:T(8,128)(2,1)S(1)}, bf16[160,1152]{1,0:T(8,128)(2,1)}, u32[]{:S(2)}) %copy-start) | copy-done | bytes 368664
  29.5 1.0 %copy-done.1 = bf16[160,1152]{1,0:T(8,128)(2,1)S(1)} copy-done((bf16[160,1152]{1,0:T(8,128)(2,1)S(1)}, bf16[160,1152]{1,0:T(8,128)(2,1)}, u32[]{:S(2)}) %copy-start.1) | copy-done | bytes 368664
  30.5 6.2 %pairs.1 = (f32[160,1152]{1,0:T(8,128)S(1)}, bf16[160,1152]{1,0:T(8,128)(2,1)S(1)}, bf16[160,1152]{1,0:T(8,128)(2,1)S(1)}, bf16[160,1152]{1,0:T(8,128)(2,1)S(1)}...) custom-call(f32[1]{0:T(128)S(6)} %copy.6.temp, ...), custom_call_target="tpu_custom_call" | custom-call | tf_op jit(solution)/shard_map/pairs/pallas_call | solution.py:118
  36.7 2.7 %collective-permute-start.10 = (bf16[160,1152]{1,0:T(8,128)(2,1)S(1)}, bf16[160,1152]{1,0:T(8,128)(2,1)S(1)}, u32[]{:S(2)}, u32[]{:S(2)}) collective-permute-start(bf16[160,1152]{1,0:T(8,128)(2,1)S(1)} %get-tuple-element.17), channel_id=1, source_target_pairs={{0,120},{8,0},{16,8},{24,16},{32,24},{40,32},{48,40},{56,48},{64,5... | collective-permute-start | bytes 1105928 | tf_op jit(solution)/shard_map/ppermute | solution.py:18
  39.4 0.3 collective-permute-start.6
  39.6 0.8 %collective-permute-start.7 = (bf16[160,1152]{1,0:T(8,128)(2,1)S(1)}, bf16[160,1152]{1,0:T(8,128)(2,1)S(1)}, u32[]{:S(2)}, u32[]{:S(2)}) collective-permute-start(bf16[160,1152]{1,0:T(8,128)(2,1)S(1)} %get-tuple-element.12), channel_id=1, source_target_pairs={{0,4},{1,5},{2,6},{3,7},{4,0},{5,1},{6,2},{7,3},{8,12},{9,13},{10,... | collective-permute-start | bytes 1105928 | tf_op jit(solution)/shard_map/ppermute | solution.py:27
  40.5 1.1 %collective-permute-start.8 = (bf16[160,1152]{1,0:T(8,128)(2,1)S(1)}, bf16[160,1152]{1,0:T(8,128)(2,1)S(1)}, u32[]{:S(2)}, u32[]{:S(2)}) collective-permute-start(bf16[160,1152]{1,0:T(8,128)(2,1)S(1)} %get-tuple-element.13), channel_id=1, source_target_pairs={{0,2},{1,3},{2,4},{3,5},{4,6},{5,7},{6,0},{7,1},{8,10},{9,11},{10,... | collective-permute-start | bytes 1105928 | tf_op jit(solution)/shard_map/ppermute | solution.py:27
  41.6 2.8 %collective-permute-done.10 = bf16[160,1152]{1,0:T(8,128)(2,1)S(1)} collective-permute-done((bf16[160,1152]{1,0:T(8,128)(2,1)S(1)}, bf16[160,1152]{1,0:T(8,128)(2,1)S(1)}, u32[]{:S(2)}, u32[]{:S(2)}) %collective-permute-start.10) | collective-permute-done | bytes 368672 | tf_op jit(solution)/shard_map/ppermute | solution.py:18
  44.4 1.2 %add_convert_fusion = bf16[160,1152]{1,0:T(8,128)(2,1)S(1)} fusion(f32[160,1152]{1,0:T(8,128)} %get-tuple-element.16, bf16[160,1152]{1,0:T(8,128)(2,1)S(1)} %collective-permute-done.10), kind=kLoop, calls=%fused_computation | loop fusion | flops 552960 | bytes 1474560 | tf_op jit(solution)/shard_map/convert_element_type | solution.py:137
  45.6 0.1 collective-permute-start.11
  45.7 5.2 %collective-permute-done.6.rest_0_ = bf16[160,1152]{1,0:T(8,128)(2,1)S(1)} collective-permute-done((bf16[160,1152]{1,0:T(8,128)(2,1)S(1)}, bf16[160,1152]{1,0:T(8,128)(2,1)S(1)}, u32[]{:S(2)}, u32[]{:S(2)}) %collective-permute-start.6) | collective-permute-done | bytes 368672 | tf_op jit(solution)/shard_map/ppermute | solution.py:27
  50.9 1.8 %collective-permute-done.7.rest_1_ = bf16[160,1152]{1,0:T(8,128)(2,1)S(1)} collective-permute-done((bf16[160,1152]{1,0:T(8,128)(2,1)S(1)}, bf16[160,1152]{1,0:T(8,128)(2,1)S(1)}, u32[]{:S(2)}, u32[]{:S(2)}) %collective-permute-start.7) | collective-permute-done | bytes 368672 | tf_op jit(solution)/shard_map/ppermute | solution.py:27
  52.7 4.9 %collective-permute-done.8.rest_2_ = bf16[160,1152]{1,0:T(8,128)(2,1)S(1)} collective-permute-done((bf16[160,1152]{1,0:T(8,128)(2,1)S(1)}, bf16[160,1152]{1,0:T(8,128)(2,1)S(1)}, u32[]{:S(2)}, u32[]{:S(2)}) %collective-permute-start.8) | collective-permute-done | bytes 368672 | tf_op jit(solution)/shard_map/ppermute | solution.py:27
  57.6 1.2 %finish.2 = bf16[160,1152]{1,0:T(8,128)(2,1)} custom-call(bf16[160,1152]{1,0:T(8,128)(2,1)S(1)} %copy-done, f32[160,1152]{1,0:T(8,128)S(1)} %get-tuple-element.10.own, bf16[160,1152]{1,0:T(8,128)(2,1)S(1)} %collective-permute-done.6.rest_0_, bf16[160,1152]{1,0:T(8,128)(2,1)S(1)} %collective-permute-done.7.rest_1_, ...), custom_call_target="tpu_custom_call" | custom-call | tf_op jit(solution)/shard_map/finish/pallas_call | solution.py:94
  58.8 0.0 copy-done.3
  58.8 1.1 %finish.3 = bf16[160,1152]{1,0:T(8,128)(2,1)} custom-call(bf16[160,1152]{1,0:T(8,128)(2,1)S(1)} %copy-done.2, f32[160,1152]{1,0:T(8,128)S(1)} %copy-done.3, bf16[160,1152]{1,0:T(8,128)(2,1)S(1)} %collective-permute-done.9.rest_0_, bf16[160,1152]{1,0:T(8,128)(2,1)S(1)} %collective-permute-done.11.rest_1_), custom_call_target="tpu_custom_call" | custom-call | tf_op jit(solution)/shard_map/finish/pallas_call | solution.py:94
  (12 shorter events, 0.0 us)
Async XLA Ops:
  0.6 16.8 %collective-permute-start.3 = (bf16[160,1152]{1,0:T(8,128)(2,1)}, bf16[160,1152]{1,0:T(8,128)(2,1)S(1)}, u32[]{:S(2)}, u32[]{:S(2)}) collective-permute-start(bf16[160,1152]{1,0:T(8,128)(2,1)} %raw.3), channel_id=1, source_target_pairs={{0,1},{1,0},{2,3},{3,2},{4,5},{5,4},{6,7},{7,6},{8,9},{9,8},{10,11... | collective-permute-start | bytes 1105928 | tf_op jit(solution)/shard_map/ppermute | solution.py:36
  4.7 14.1 %collective-permute-start.4 = (bf16[160,1152]{1,0:T(8,128)(2,1)}, bf16[160,1152]{1,0:T(8,128)(2,1)S(1)}, u32[]{:S(2)}, u32[]{:S(2)}) collective-permute-start(bf16[160,1152]{1,0:T(8,128)(2,1)} %raw.3), channel_id=1, source_target_pairs={{0,8},{8,16},{16,24},{24,32},{32,40},{40,48},{48,56},{56,64},{64,7... | collective-permute-start | bytes 1105928 | tf_op jit(solution)/shard_map/ppermute | solution.py:18
  4.7 19.1 %collective-permute-start.2 = (bf16[160,1152]{1,0:T(8,128)(2,1)}, bf16[160,1152]{1,0:T(8,128)(2,1)S(1)}, u32[]{:S(2)}, u32[]{:S(2)}) collective-permute-start(bf16[160,1152]{1,0:T(8,128)(2,1)} %raw.2), channel_id=1, source_target_pairs={{0,6},{1,7},{2,0},{3,1},{4,2},{5,3},{6,4},{7,5},{8,14},{9,15},{10,... | collective-permute-start | bytes 1105928 | tf_op jit(solution)/shard_map/ppermute | solution.py:27
  7.4 16.4 %collective-permute-start.1 = (bf16[160,1152]{1,0:T(8,128)(2,1)}, bf16[160,1152]{1,0:T(8,128)(2,1)S(1)}, u32[]{:S(2)}, u32[]{:S(2)}) collective-permute-start(bf16[160,1152]{1,0:T(8,128)(2,1)} %raw.2), channel_id=1, source_target_pairs={{0,4},{1,5},{2,6},{3,7},{4,0},{5,1},{6,2},{7,3},{8,12},{9,13},{10,... | collective-permute-start | bytes 1105928 | tf_op jit(solution)/shard_map/ppermute | solution.py:27
  8.2 20.3 %collective-permute-start = (bf16[160,1152]{1,0:T(8,128)(2,1)}, bf16[160,1152]{1,0:T(8,128)(2,1)S(1)}, u32[]{:S(2)}, u32[]{:S(2)}) collective-permute-start(bf16[160,1152]{1,0:T(8,128)(2,1)} %raw.2), channel_id=1, source_target_pairs={{0,2},{1,3},{2,4},{3,5},{4,6},{5,7},{6,0},{7,1},{8,10},{9,11},{10,... | collective-permute-start | bytes 1105928 | tf_op jit(solution)/shard_map/ppermute | solution.py:27
  17.4 11.1 %collective-permute-start.5 = (bf16[160,1152]{1,0:T(8,128)(2,1)S(1)}, bf16[160,1152]{1,0:T(8,128)(2,1)S(1)}, u32[]{:S(2)}, u32[]{:S(2)}) collective-permute-start(bf16[160,1152]{1,0:T(8,128)(2,1)S(1)} %collective-permute-done.3.t1), channel_id=1, source_target_pairs={{0,8},{8,16},{16,24},{24,32},{32,40},{40,48},{48,56},{56,64},{64,7... | collective-permute-start | bytes 1105928 | tf_op jit(solution)/shard_map/ppermute | solution.py:18
  28.5 1.0 %copy-start = (bf16[160,1152]{1,0:T(8,128)(2,1)S(1)}, bf16[160,1152]{1,0:T(8,128)(2,1)}, u32[]{:S(2)}) copy-start(bf16[160,1152]{1,0:T(8,128)(2,1)} %raw.2) | copy-start | bytes 1105924
  29.5 1.0 %copy-start.1 = (bf16[160,1152]{1,0:T(8,128)(2,1)S(1)}, bf16[160,1152]{1,0:T(8,128)(2,1)}, u32[]{:S(2)}) copy-start(bf16[160,1152]{1,0:T(8,128)(2,1)} %raw.3) | copy-start | bytes 1105924
  36.7 7.7 %collective-permute-start.10 = (bf16[160,1152]{1,0:T(8,128)(2,1)S(1)}, bf16[160,1152]{1,0:T(8,128)(2,1)S(1)}, u32[]{:S(2)}, u32[]{:S(2)}) collective-permute-start(bf16[160,1152]{1,0:T(8,128)(2,1)S(1)} %get-tuple-element.17), channel_id=1, source_target_pairs={{0,120},{8,0},{16,8},{24,16},{32,24},{40,32},{48,40},{56,48},{64,5... | collective-permute-start | bytes 1105928 | tf_op jit(solution)/shard_map/ppermute | solution.py:18
  39.4 11.5 %collective-permute-start.6 = (bf16[160,1152]{1,0:T(8,128)(2,1)S(1)}, bf16[160,1152]{1,0:T(8,128)(2,1)S(1)}, u32[]{:S(2)}, u32[]{:S(2)}) collective-permute-start(bf16[160,1152]{1,0:T(8,128)(2,1)S(1)} %get-tuple-element.11), channel_id=1, source_target_pairs={{0,6},{1,7},{2,0},{3,1},{4,2},{5,3},{6,4},{7,5},{8,14},{9,15},{10,... | collective-permute-start | bytes 1105928 | tf_op jit(solution)/shard_map/ppermute | solution.py:27
  39.6 13.0 %collective-permute-start.7 = (bf16[160,1152]{1,0:T(8,128)(2,1)S(1)}, bf16[160,1152]{1,0:T(8,128)(2,1)S(1)}, u32[]{:S(2)}, u32[]{:S(2)}) collective-permute-start(bf16[160,1152]{1,0:T(8,128)(2,1)S(1)} %get-tuple-element.12), channel_id=1, source_target_pairs={{0,4},{1,5},{2,6},{3,7},{4,0},{5,1},{6,2},{7,3},{8,12},{9,13},{10,... | collective-permute-start | bytes 1105928 | tf_op jit(solution)/shard_map/ppermute | solution.py:27
  40.5 17.1 %collective-permute-start.8 = (bf16[160,1152]{1,0:T(8,128)(2,1)S(1)}, bf16[160,1152]{1,0:T(8,128)(2,1)S(1)}, u32[]{:S(2)}, u32[]{:S(2)}) collective-permute-start(bf16[160,1152]{1,0:T(8,128)(2,1)S(1)} %get-tuple-element.13), channel_id=1, source_target_pairs={{0,2},{1,3},{2,4},{3,5},{4,6},{5,7},{6,0},{7,1},{8,10},{9,11},{10,... | collective-permute-start | bytes 1105928 | tf_op jit(solution)/shard_map/ppermute | solution.py:27
  41.6 17.2 %collective-permute-start.9 = (bf16[160,1152]{1,0:T(8,128)(2,1)S(1)}, bf16[160,1152]{1,0:T(8,128)(2,1)S(1)}, u32[]{:S(2)}, u32[]{:S(2)}) collective-permute-start(bf16[160,1152]{1,0:T(8,128)(2,1)S(1)} %get-tuple-element.15), channel_id=1, source_target_pairs={{0,120},{8,0},{16,8},{24,16},{32,24},{40,32},{48,40},{56,48},{64,5... | collective-permute-start | bytes 1105928 | tf_op jit(solution)/shard_map/ppermute | solution.py:18
  45.6 13.2 %collective-permute-start.11 = (bf16[160,1152]{1,0:T(8,128)(2,1)S(1)}, bf16[160,1152]{1,0:T(8,128)(2,1)S(1)}, u32[]{:S(2)}, u32[]{:S(2)}) collective-permute-start(bf16[160,1152]{1,0:T(8,128)(2,1)S(1)} %add_convert_fusion), channel_id=1, source_target_pairs={{0,1},{1,0},{2,3},{3,2},{4,5},{5,4},{6,7},{7,6},{8,9},{9,8},{10,11... | collective-permute-start | bytes 1105928 | tf_op jit(solution)/shard_map/ppermute | solution.py:36
  57.6 1.2 %copy-start.2 = (bf16[160,1152]{1,0:T(8,128)(2,1)S(1)}, bf16[160,1152]{1,0:T(8,128)(2,1)}, u32[]{:S(2)}) copy-start(bf16[160,1152]{1,0:T(8,128)(2,1)} %raw.3) | copy-start | bytes 1105924
  57.6 1.2 %copy-start.3 = (f32[160,1152]{1,0:T(8,128)S(1)}, f32[160,1152]{1,0:T(8,128)}, u32[]{:S(2)}) copy-start(f32[160,1152]{1,0:T(8,128)} %get-tuple-element.14.own) | copy-start | bytes 2211844

commit v2 on v1

v2 whole, which is shorter than its diff:
```python
import jax
import jax.numpy as jnp
from jax import lax
from jax.experimental import pallas as pl
from jax.experimental.pallas import tpu as pltpu
from jax.sharding import PartitionSpec as P

VMEM = pltpu.VMEM
LIMIT = 40 * 1024 * 1024
BLK_X = 4
BLK_Z = 2
BF16 = jnp.bfloat16
F32 = jnp.float32


def shift_prev(value, steps):
    count = lax.axis_size("outer")
    return lax.ppermute(value, "outer", [(s, (s + steps) % count) for s in range(count)])


def shift_x(value, steps):
    pairs = [
        (x * BLK_Z + z, (x + steps) % BLK_X * BLK_Z + z)
        for x in range(BLK_X)
        for z in range(BLK_Z)
    ]
    return lax.ppermute(value, "blk", pairs)


def shift_around(value):
    outer, blk = lax.axis_size("outer"), lax.axis_size("blk")
    pairs = []
    for s in range(outer):
        for b in range(blk):
            x = (b // BLK_Z + 1 - s % 2 * 2) % BLK_X
            pairs.append((s * blk + b, s * blk + x * BLK_Z + b % BLK_Z))
    return lax.ppermute(value, ("outer", "blk"), pairs)


def swap_z(value):
    pairs = [
        (x * BLK_Z + z, x * BLK_Z + (BLK_Z - 1 - z))
        for x in range(BLK_X)
        for z in range(BLK_Z)
    ]
    return lax.ppermute(value, "blk", pairs)


def call(body, name, outs, flops, operands, scratch=(), smem=0, aliases=None):
    specs = [pl.BlockSpec(memory_space=pltpu.SMEM)] * smem
    specs += [pl.BlockSpec(memory_space=VMEM)] * (len(operands) - smem)
    size = sum(v.size * v.dtype.itemsize for v in operands)
    return pl.pallas_call(
        body,
        out_shape=outs,
        in_specs=specs,
        out_specs=[pl.BlockSpec(memory_space=VMEM)] * len(outs),
        scratch_shapes=list(scratch),
        input_output_aliases=aliases or {},
        compiler_params=pltpu.CompilerParams(vmem_limit_bytes=LIMIT),
        cost_estimate=pl.CostEstimate(flops=flops, bytes_accessed=0, transcendentals=0),
        name=name,
    )(*operands)


def normalized(ref):
    values = ref[...].astype(F32)
    length = jnp.sqrt(jnp.sum(values * values, axis=-1, keepdims=True) + 1e-06)
    return (values / length).astype(BF16)


def scores(left, right):
    return lax.dot_general(left, right, (((1,), (1,)), ((), ())), preferred_element_type=F32)


def sums(left, right):
    return lax.dot_general(left, right, (((0,), (0,)), ((), ())), preferred_element_type=F32)


def near_units_kernel(core, temp, bias, x1_raw, x3_raw, pair, sent):
    rows = sent.shape[0]
    pair[:rows, :] = normalized(x1_raw)
    pair[rows:, :] = normalized(x3_raw)

    @pl.when(core[0] == 0)
    def _():
        sent[...] = pair[:rows, :]

    @pl.when(core[0] != 0)
    def _():
        sent[...] = pair[rows:, :]


def early_kernel(temp, bias, images, texts, part_raw, p0_raw, pair, img, txt, sig):
    rows = images.shape[0]
    img[:rows, :] = normalized(images)
    img[rows : 3 * rows, :] = pair[...]
    for k, raw in enumerate((texts, part_raw, p0_raw)):
        txt[k * rows : (k + 1) * rows, :] = normalized(raw)
    early = 3 * rows
    value = jax.nn.sigmoid(temp[0] * scores(img[:early, :], txt[:early, :]) + bias[0])
    row = lax.broadcasted_iota(jnp.int32, value.shape, 0)
    col = lax.broadcasted_iota(jnp.int32, value.shape, 1)
    same = jnp.logical_and(row == col, row < rows)
    sig[:early, :early] = (value - same.astype(F32)).astype(BF16)


def late_kernel(
    temp, bias, p1_raw, x2, img_in, txt_in, sig_in, img, txt, sig, d1, d3, d2
):
    rows = p1_raw.shape[0]
    early = 3 * rows
    txt[early:, :] = normalized(p1_raw)
    img[early:, :] = x2[...]
    value = jax.nn.sigmoid(temp[0] * scores(img[early:, :], txt[...]) + bias[0])
    sig[early:, :] = value.astype(BF16)
    value = jax.nn.sigmoid(temp[0] * scores(img[:early, :], txt[early:, :]) + bias[0])
    sig[:early, early:] = value.astype(BF16)
    for k, out in ((1, d1), (2, d3), (3, d2)):
        weight = sig[k * rows : (k + 1) * rows, :]
        total = jnp.dot(weight, txt[...], preferred_element_type=F32)
        out[...] = (temp[0] * total).astype(BF16)


def middle_kernel(
    temp, bias, img, txt, sig, n0_raw, n_pair, d0, e_own, e_part, nxt, sig_next
):
    rows = d0.shape[0]
    early = 3 * rows
    d0[...] = temp[0] * jnp.dot(sig[:rows, :], txt[...], preferred_element_type=F32)
    e_own[...] = temp[0] * sums(sig[:, :rows], img[...])
    e_part[...] = temp[0] * sums(sig[:, rows : 2 * rows], img[...])
    nxt[:rows, :] = normalized(n0_raw)
    nxt[rows:early, :] = n_pair[...]
    value = scores(nxt[:early, :], txt[: 2 * rows, :])
    sig_next[:early, :] = jax.nn.sigmoid(temp[0] * value + bias[0]).astype(BF16)


def part_kernel(temp, bias, n2, txt, e_part, nxt_in, sig_in, nxt, sig_next, to_part):
    rows = n2.shape[0]
    early = 3 * rows
    nxt[early:, :] = n2[...]
    value = scores(nxt[early:, :], txt[: 2 * rows, :])
    sig_next[early:, :] = jax.nn.sigmoid(temp[0] * value + bias[0]).astype(BF16)
    total = e_part[...] + temp[0] * sums(sig_next[:, rows:], nxt[...])
    to_part[...] = total.astype(BF16)


def own_kernel(temp, e_own, nxt, sig_next, out):
    rows = out.shape[0]
    out[...] = e_own[...] + temp[0] * sums(sig_next[:, :rows], nxt[...])


def finish_kernel(raw, own, *rest):
    out = rest[-1]
    values = raw[...].astype(F32)
    length = jnp.sqrt(jnp.sum(values * values, axis=-1, keepdims=True) + 1e-06)
    unit = values / length
    total = own[...]
    for ref in rest[:-1]:
        total = total + ref[...].astype(F32)
    inner = jnp.sum(unit * total, axis=-1, keepdims=True)
    out[...] = ((total - unit * inner) / length).astype(out.dtype)


def local(images, texts, temp, bias):
    shape = images.shape
    rows, width = shape
    many = 4 * rows
    tile = 2 * rows * rows * width
    f32 = jax.ShapeDtypeStruct(shape, F32)
    b16 = jax.ShapeDtypeStruct(shape, BF16)
    stack = jax.ShapeDtypeStruct((many, width), BF16)
    sigs = jax.ShapeDtypeStruct((many, many), BF16)
    halves = jax.ShapeDtypeStruct((many, 2 * rows), BF16)
    wide = jax.ShapeDtypeStruct((2 * rows, width), BF16)
    core = (lax.axis_index("outer") % 2).astype(jnp.int32).reshape(1)

    part_raw = swap_z(texts)
    x1_raw = shift_x(images, 1)
    x3_raw = shift_x(images, -1)
    p0_raw = shift_prev(texts, 1)
    p1_raw = shift_prev(part_raw, 1)
    n0_raw = shift_prev(images, -1)
    pair, sent = call(
        near_units_kernel, "units_near", [wide, b16], 3000000000, (core, temp, bias, x1_raw, x3_raw), smem=3
    )
    x2 = shift_around(sent)
    n_pair = shift_prev(pair, -1)
    n2 = shift_prev(x2, -1)

    img, txt, sig = call(
        early_kernel, "early_pairs", [stack, stack, sigs], 1000000000,
        (temp, bias, images, texts, part_raw, p0_raw, pair), smem=2,
    )
    img, txt, sig, d1, d3, d2 = call(
        late_kernel, "late_pairs", [stack, stack, sigs] + [b16] * 3, 10000000,
        (temp, bias, p1_raw, x2, img, txt, sig), smem=2, aliases={4: 0, 5: 1, 6: 2},
    )
    r1 = shift_x(d1, -1)
    r3 = shift_x(d3, 1)
    r2 = shift_x(d2, 2)
    d0, e_own, e_part, nxt, sig_next = call(
        middle_kernel, "middle_sums", [f32] * 3 + [stack, halves], 0,
        (temp, bias, img, txt, sig, n0_raw, n_pair), smem=2,
    )
    nxt, sig_next, to_part = call(
        part_kernel, "part_sums", [stack, halves, b16], 100000000,
        (temp, bias, n2, txt, e_part, nxt, sig_next), smem=2, aliases={5: 0, 6: 1},
    )
    from_part = swap_z(to_part)
    (e_own,) = call(own_kernel, "own_sums", [f32], 1000000000, (temp, e_own, nxt, sig_next), smem=1)
    (grad_images,) = call(
        finish_kernel, "finish_images", [b16], 100000000000, (images, d0, r1, r3, r2)
    )
    (grad_texts,) = call(
        finish_kernel, "finish_texts", [b16], 100000000, (texts, e_own, from_part)
    )
    return (grad_images, grad_texts)


def solution(mesh):
    spec = P(("outer", "blk"), None)
    return jax.shard_map(
        local,
        mesh=mesh,
        in_specs=(spec, spec, P(), P()),
        out_specs=(spec, spec),
        check_vma=False,
    )
```

time: 61.1 us -> 50.4 us (0.82); the launches traced: 59.9 us -> 49.8 us
  waiting for transfers between devices: 32.7 us -> 11.9 us
  starting transfers between devices: 13.5 us -> 26.1 us
  local copies, waits for them, and re-layouts: 2.02 us -> 0.01 us
  Pallas kernels: 8.52 us -> 9.88 us
  other arithmetic: 1.18 us -> 0 us
    ppermute x6 -> x5, waiting for transfers between devices: 21.6 us -> 8.45 us  [shift_x(): return lax.ppermute(value, 'blk', pairs)]
    ppermute x2, waiting for transfers between devices: 8.3 us -> 0.01 us  [swap_z(): return lax.ppermute(value, 'blk', pairs)]
    ppermute x4 -> x5, starting transfers between devices: 2.66 us -> 8.24 us  [shift_prev(): lax.ppermute(value, 'outer', [(s, (s + steps) % count) for s in range(cou...]
    ppermute x2, starting transfers between devices: 4.18 us -> 8.04 us  [swap_z(): return lax.ppermute(value, 'blk', pairs)]
    unnamed x8 -> x4, local copies, waits for them, and re-layouts: 2.02 us -> 0.01 us
    ppermute x0 -> x1, starting transfers between devices: none -> 1.56 us  [shift_around(): return lax.ppermute(value, ('outer', 'blk'), pairs)]
    ppermute x6 -> x5, starting transfers between devices: 6.67 us -> 8.22 us  [shift_x(): return lax.ppermute(value, 'blk', pairs)]
    pallas_call x3 -> x8, Pallas kernels: 8.52 us -> 9.88 us  [call(): pl.pallas_call(body, out_shape=outs, in_specs=specs, out_specs=[pl.BlockS...]
  transfers between devices with their start and end apart: 12 -> 13, of which waited for: 7 -> 7; matrix products, arithmetic and copies ran while one was open for 2% -> 0% of each run, Pallas kernels for 2% -> 18%
where the time goes in v2:
time: 50.4 us; the launch traced here: 49.8 us
  starting transfers between devices  26.1 us (52%)
  waiting for transfers between devices  11.9 us (24%)
  Pallas kernels  9.88 us (20%)
  between operations  2.01 us (4%)
    pallas_call x8, Pallas kernels, call(): pl.pallas_call(body, out_shape=outs, in_specs=specs, out_specs=[pl.BlockS...  9.88 us
    ppermute x5, waiting for transfers between devices, shift_x(): return lax.ppermute(value, 'blk', pairs)  8.45 us
    ppermute x5, starting transfers between devices, shift_prev(): lax.ppermute(value, 'outer', [(s, (s + steps) % count) for s in range(cou...  8.24 us
    ppermute x5, starting transfers between devices, shift_x(): return lax.ppermute(value, 'blk', pairs)  8.22 us
    ppermute x2, starting transfers between devices, swap_z(): return lax.ppermute(value, 'blk', pairs)  8.04 us
    ppermute x5, waiting for transfers between devices, shift_prev(): lax.ppermute(value, 'outer', [(s, (s + steps) % count) for s in range(cou...  3.4 us
    ppermute x1, starting transfers between devices, shift_around(): return lax.ppermute(value, ('outer', 'blk'), pairs)  1.56 us
  transfers between devices with their start and end apart: 13, of which 7 were waited for; matrix products, arithmetic and copies ran while one was open for 0% of the time, Pallas kernels for 18%

profile of v2, /device:TPU:0, one launch (start us, length us, event | category | flops | bytes accessed | tf_op | source)
XLA Modules:
  0.0 49.8 jit_solution(9133223432894129496)
XLA Ops:
  0.6 1.6 %collective-permute-start.2 = (bf16[160,1152]{1,0:T(8,128)(2,1)}, bf16[160,1152]{1,0:T(8,128)(2,1)S(1)}, u32[]{:S(2)}, u32[]{:S(2)}) collective-permute-start(bf16[160,1152]{1,0:T(8,128)(2,1)} %raw.2), channel_id=1, source_target_pairs={{0,2},{1,3},{2,4},{3,5},{4,6},{5,7},{6,0},{7,1},{8,10},{9,11},{10,... | collective-permute-start | bytes 1105928 | tf_op jit(solution)/shard_map/ppermute | solution.py:27
  2.3 1.7 %collective-permute-start.3 = (bf16[160,1152]{1,0:T(8,128)(2,1)}, bf16[160,1152]{1,0:T(8,128)(2,1)S(1)}, u32[]{:S(2)}, u32[]{:S(2)}) collective-permute-start(bf16[160,1152]{1,0:T(8,128)(2,1)} %raw.2), channel_id=1, source_target_pairs={{0,6},{1,7},{2,0},{3,1},{4,2},{5,3},{6,4},{7,5},{8,14},{9,15},{10,... | collective-permute-start | bytes 1105928 | tf_op jit(solution)/shard_map/ppermute | solution.py:27
  3.9 4.0 %collective-permute-start = (bf16[160,1152]{1,0:T(8,128)(2,1)}, bf16[160,1152]{1,0:T(8,128)(2,1)S(1)}, u32[]{:S(2)}, u32[]{:S(2)}) collective-permute-start(bf16[160,1152]{1,0:T(8,128)(2,1)} %raw.3), channel_id=1, source_target_pairs={{0,1},{1,0},{2,3},{3,2},{4,5},{5,4},{6,7},{7,6},{8,9},{9,8},{10,11... | collective-permute-start | bytes 1105928 | tf_op jit(solution)/shard_map/ppermute | solution.py:46
  9.2 3.1 %collective-permute-done.2.x1_raw = bf16[160,1152]{1,0:T(8,128)(2,1)S(1)} collective-permute-done((bf16[160,1152]{1,0:T(8,128)(2,1)}, bf16[160,1152]{1,0:T(8,128)(2,1)S(1)}, u32[]{:S(2)}, u32[]{:S(2)}) %collective-permute-start.2) | collective-permute-done | bytes 368672 | tf_op jit(solution)/shard_map/ppermute | solution.py:27
  12.9 1.6 %collective-permute-start.4 = (bf16[160,1152]{1,0:T(8,128)(2,1)S(1)}, bf16[160,1152]{1,0:T(8,128)(2,1)S(1)}, u32[]{:S(2)}, u32[]{:S(2)}) collective-permute-start(bf16[160,1152]{1,0:T(8,128)(2,1)S(1)} %get-tuple-element.21), channel_id=1, source_target_pairs={{0,2},{1,3},{2,4},{3,5},{4,6},{5,7},{6,0},{7,1},{8,14},{9,15},{10,... | collective-permute-start | bytes 1105928 | tf_op jit(solution)/shard_map/ppermute | solution.py:37
  14.4 3.9 %collective-permute-start.7 = (bf16[320,1152]{1,0:T(8,128)(2,1)S(1)}, bf16[320,1152]{1,0:T(8,128)(2,1)S(1)}, u32[]{:S(2)}, u32[]{:S(2)}) collective-permute-start(bf16[320,1152]{1,0:T(8,128)(2,1)S(1)} %get-tuple-element.22.pair), channel_id=1, source_target_pairs={{0,120},{8,0},{16,8},{24,16},{32,24},{40,32},{48,40},{56,48},{64,5... | collective-permute-start | bytes 2211848 | tf_op jit(solution)/shard_map/ppermute | solution.py:18
  18.3 3.9 %collective-permute-start.6 = (bf16[160,1152]{1,0:T(8,128)(2,1)S(1)}, bf16[160,1152]{1,0:T(8,128)(2,1)S(1)}, u32[]{:S(2)}, u32[]{:S(2)}) collective-permute-start(bf16[160,1152]{1,0:T(8,128)(2,1)S(1)} %copy-done.1), channel_id=1, source_target_pairs={{0,120},{8,0},{16,8},{24,16},{32,24},{40,32},{48,40},{56,48},{64,5... | collective-permute-start | bytes 1105928 | tf_op jit(solution)/shard_map/ppermute | solution.py:18
  22.1 0.5 %collective-permute-start.11 = (bf16[160,1152]{1,0:T(8,128)(2,1)S(1)}, bf16[160,1152]{1,0:T(8,128)(2,1)S(1)}, u32[]{:S(2)}, u32[]{:S(2)}) collective-permute-start(bf16[160,1152]{1,0:T(8,128)(2,1)S(1)} %collective-permute-done.4.x2), channel_id=1, source_target_pairs={{0,120},{8,0},{16,8},{24,16},{32,24},{40,32},{48,40},{56,48},{64,5... | collective-permute-start | bytes 1105928 | tf_op jit(solution)/shard_map/ppermute | solution.py:18
  22.7 0.8 %collective-permute-done.5.p0_raw = bf16[160,1152]{1,0:T(8,128)(2,1)S(1)} collective-permute-done((bf16[160,1152]{1,0:T(8,128)(2,1)S(1)}, bf16[160,1152]{1,0:T(8,128)(2,1)S(1)}, u32[]{:S(2)}, u32[]{:S(2)}) %collective-permute-start.5) | collective-permute-done | bytes 368672 | tf_op jit(solution)/shard_map/ppermute | solution.py:18
  23.5 1.3 %early_pairs.1 = (bf16[640,1152]{1,0:T(8,128)(2,1)S(1)}, bf16[640,1152]{1,0:T(8,128)(2,1)S(1)}, bf16[640,640]{1,0:T(8,128)(2,1)S(1)}) custom-call(f32[1]{0:T(128)S(6)} %copy.16.temp, f32[1]{0:T(128)S(6)} %copy.17.bias, bf16[160,1152]{1,0:T(8,128)(2,1)S(1)} %copy-done.1, bf16[160,1152]{1,0:T(8,128)(2,1)S(1)} %copy-done, ...), custom_call_target="tpu_custom_call" | custom-call | flops 1000000000 | tf_op jit(solution)/shard_map/early_pairs/pallas_call | solution.py:53
  24.8 2.6 %collective-permute-done.1.p1_raw = bf16[160,1152]{1,0:T(8,128)(2,1)S(1)} collective-permute-done((bf16[160,1152]{1,0:T(8,128)(2,1)S(1)}, bf16[160,1152]{1,0:T(8,128)(2,1)S(1)}, u32[]{:S(2)}, u32[]{:S(2)}) %collective-permute-start.1) | collective-permute-done | bytes 368672 | tf_op jit(solution)/shard_map/ppermute | solution.py:18
  27.4 2.6 %late_pairs.1 = (bf16[640,1152]{1,0:T(8,128)(2,1)S(1)}, bf16[640,1152]{1,0:T(8,128)(2,1)S(1)}, bf16[640,640]{1,0:T(8,128)(2,1)S(1)}, bf16[160,1152]{1,0:T(8,128)...) custom-call(f32[1]{0:T(128)S(6)} %copy.16.temp, ...), custom_call_target="tpu_custom_call", output_to_operand_aliasing={{0}: (4, {}), {1}: (5, {}), {2}: (6, {})} | custom-call | flops 10000000 | tf_op jit(solution)/shard_map/late_pairs/pallas_call | solution.py:53
  30.0 2.9 %collective-permute-start.10 = (bf16[160,1152]{1,0:T(8,128)(2,1)S(1)}, bf16[160,1152]{1,0:T(8,128)(2,1)S(1)}, u32[]{:S(2)}, u32[]{:S(2)}) collective-permute-start(bf16[160,1152]{1,0:T(8,128)(2,1)S(1)} %get-tuple-element.32), channel_id=1, source_target_pairs={{0,4},{1,5},{2,6},{3,7},{4,0},{5,1},{6,2},{7,3},{8,12},{9,13},{10,... | collective-permute-start | bytes 1105928 | tf_op jit(solution)/shard_map/ppermute | solution.py:27
  32.9 1.1 %collective-permute-start.8 = (bf16[160,1152]{1,0:T(8,128)(2,1)S(1)}, bf16[160,1152]{1,0:T(8,128)(2,1)S(1)}, u32[]{:S(2)}, u32[]{:S(2)}) collective-permute-start(bf16[160,1152]{1,0:T(8,128)(2,1)S(1)} %get-tuple-element.30), channel_id=1, source_target_pairs={{0,6},{1,7},{2,0},{3,1},{4,2},{5,3},{6,4},{7,5},{8,14},{9,15},{10,... | collective-permute-start | bytes 1105928 | tf_op jit(solution)/shard_map/ppermute | solution.py:27
  33.9 1.0 %collective-permute-start.9 = (bf16[160,1152]{1,0:T(8,128)(2,1)S(1)}, bf16[160,1152]{1,0:T(8,128)(2,1)S(1)}, u32[]{:S(2)}, u32[]{:S(2)}) collective-permute-start(bf16[160,1152]{1,0:T(8,128)(2,1)S(1)} %get-tuple-element.31), channel_id=1, source_target_pairs={{0,2},{1,3},{2,4},{3,5},{4,6},{5,7},{6,0},{7,1},{8,10},{9,11},{10,... | collective-permute-start | bytes 1105928 | tf_op jit(solution)/shard_map/ppermute | solution.py:27
  34.9 1.8 %middle_sums.1 = (f32[160,1152]{1,0:T(8,128)S(1)}, f32[160,1152]{1,0:T(8,128)S(1)}, f32[160,1152]{1,0:T(8,128)S(1)}, bf16[640,1152]{1,0:T(8,128)(2,1)S(1)}, bf16[640,320]{1,0:T(8,128)(2,1)S(1)}) custom-call(f32[1]{0:T(128)S(6)} %copy.16.temp, f32[1]{0:T(128)S(6)} %copy.17.bias, bf16[640,1152]{1,0:T(8,128)(2,1)S(1)} %get-tuple-element.26.img, ...), custom_call_target="tpu_custom_call" | custom-call | tf_op jit(solution)/shard_map/middle_sums/pallas_call | solution.py:53
  36.7 1.1 %part_sums.1 = (bf16[640,1152]{1,0:T(8,128)(2,1)S(1)}, bf16[640,320]{1,0:T(8,128)(2,1)S(1)}, bf16[160,1152]{1,0:T(8,128)(2,1)S(1)}) custom-call(f32[1]{0:T(128)S(6)} %copy.16.temp, f32[1]{0:T(128)S(6)} %copy.17.bias, bf16[160,1152]{1,0:T(8,128)(2,1)S(1)} %collective-permute-done.11.n2, ...), custom_call_target="tpu_custom_call", output_to_operand_aliasing={{0}: (5, {}), {1}: (6, {})} | custom-call | flops 100000000 | tf_op jit(solution)/shard_map/part_sums/pallas_call | solution.py:53
  37.9 4.1 %collective-permute-start.12 = (bf16[160,1152]{1,0:T(8,128)(2,1)S(1)}, bf16[160,1152]{1,0:T(8,128)(2,1)S(1)}, u32[]{:S(2)}, u32[]{:S(2)}) collective-permute-start(bf16[160,1152]{1,0:T(8,128)(2,1)S(1)} %get-tuple-element.39), channel_id=1, source_target_pairs={{0,1},{1,0},{2,3},{3,2},{4,5},{5,4},{6,7},{7,6},{8,9},{9,8},{10,11... | collective-permute-start | bytes 1105928 | tf_op jit(solution)/shard_map/ppermute | solution.py:46
  41.9 1.1 %collective-permute-done.10.rest_2_ = bf16[160,1152]{1,0:T(8,128)(2,1)S(1)} collective-permute-done((bf16[160,1152]{1,0:T(8,128)(2,1)S(1)}, bf16[160,1152]{1,0:T(8,128)(2,1)S(1)}, u32[]{:S(2)}, u32[]{:S(2)}) %collective-permute-start.10) | collective-permute-done | bytes 368672 | tf_op jit(solution)/shard_map/ppermute | solution.py:27
  43.1 3.4 %collective-permute-done.8.rest_0_ = bf16[160,1152]{1,0:T(8,128)(2,1)S(1)} collective-permute-done((bf16[160,1152]{1,0:T(8,128)(2,1)S(1)}, bf16[160,1152]{1,0:T(8,128)(2,1)S(1)}, u32[]{:S(2)}, u32[]{:S(2)}) %collective-permute-start.8) | collective-permute-done | bytes 368672 | tf_op jit(solution)/shard_map/ppermute | solution.py:27
  46.5 0.6 %collective-permute-done.9.rest_1_ = bf16[160,1152]{1,0:T(8,128)(2,1)S(1)} collective-permute-done((bf16[160,1152]{1,0:T(8,128)(2,1)S(1)}, bf16[160,1152]{1,0:T(8,128)(2,1)S(1)}, u32[]{:S(2)}, u32[]{:S(2)}) %collective-permute-start.9) | collective-permute-done | bytes 368672 | tf_op jit(solution)/shard_map/ppermute | solution.py:27
  47.1 1.2 %finish_images.1 = bf16[160,1152]{1,0:T(8,128)(2,1)} custom-call(bf16[160,1152]{1,0:T(8,128)(2,1)S(1)} %copy-done.1, f32[160,1152]{1,0:T(8,128)S(1)} %get-tuple-element.29.own, bf16[160,1152]{1,0:T(8,128)(2,1)S(1)} %collective-permute-done.8.rest_0_, bf16[160,1152]{1,0:T(8,128)(2,1)S(1)} %collective-permute-done.9.rest_1_, ...), custom_call_target="tpu_custom_call" | custom-call | flops 99999997952 | tf_op jit(solution)/shard_map/finish_images/pallas_call | solution.py:53
  48.2 0.5 %own_sums.1.own = f32[160,1152]{1,0:T(8,128)S(1)} custom-call(f32[1]{0:T(128)S(6)} %copy.16.temp, f32[160,1152]{1,0:T(8,128)S(1)} %get-tuple-element.33.e_own, bf16[640,1152]{1,0:T(8,128)(2,1)S(1)} %get-tuple-element.37.nxt, bf16[640,320]{1,0:T(8,128)(2,1)S(1)} %get-tuple-element.38.sig_next), custom_call_target="tpu_custom_call" | custom-call | flops 1000000000 | tf_op jit(solution)/shard_map/own_sums/pallas_call | solution.py:53
  48.8 1.1 %finish_texts.1 = bf16[160,1152]{1,0:T(8,128)(2,1)} custom-call(bf16[160,1152]{1,0:T(8,128)(2,1)S(1)} %copy-done, f32[160,1152]{1,0:T(8,128)S(1)} %own_sums.1.own, bf16[160,1152]{1,0:T(8,128)(2,1)S(1)} %collective-permute-done.12.rest_0_), custom_call_target="tpu_custom_call" | custom-call | flops 100000000 | tf_op jit(solution)/shard_map/finish_texts/pallas_call | solution.py:53
  (14 shorter events, 0.5 us)
Async XLA Ops:
  0.6 11.7 %collective-permute-start.2 = (bf16[160,1152]{1,0:T(8,128)(2,1)}, bf16[160,1152]{1,0:T(8,128)(2,1)S(1)}, u32[]{:S(2)}, u32[]{:S(2)}) collective-permute-start(bf16[160,1152]{1,0:T(8,128)(2,1)} %raw.2), channel_id=1, source_target_pairs={{0,2},{1,3},{2,4},{3,5},{4,6},{5,7},{6,0},{7,1},{8,10},{9,11},{10,... | collective-permute-start | bytes 1105928 | tf_op jit(solution)/shard_map/ppermute | solution.py:27
  2.3 10.3 %collective-permute-start.3 = (bf16[160,1152]{1,0:T(8,128)(2,1)}, bf16[160,1152]{1,0:T(8,128)(2,1)S(1)}, u32[]{:S(2)}, u32[]{:S(2)}) collective-permute-start(bf16[160,1152]{1,0:T(8,128)(2,1)} %raw.2), channel_id=1, source_target_pairs={{0,6},{1,7},{2,0},{3,1},{4,2},{5,3},{6,4},{7,5},{8,14},{9,15},{10,... | collective-permute-start | bytes 1105928 | tf_op jit(solution)/shard_map/ppermute | solution.py:27
  3.9 14.3 %collective-permute-start = (bf16[160,1152]{1,0:T(8,128)(2,1)}, bf16[160,1152]{1,0:T(8,128)(2,1)S(1)}, u32[]{:S(2)}, u32[]{:S(2)}) collective-permute-start(bf16[160,1152]{1,0:T(8,128)(2,1)} %raw.3), channel_id=1, source_target_pairs={{0,1},{1,0},{2,3},{3,2},{4,5},{5,4},{6,7},{7,6},{8,9},{9,8},{10,11... | collective-permute-start | bytes 1105928 | tf_op jit(solution)/shard_map/ppermute | solution.py:46
  12.5 1.9 %copy-start = (bf16[160,1152]{1,0:T(8,128)(2,1)S(1)}, bf16[160,1152]{1,0:T(8,128)(2,1)}, u32[]{:S(2)}) copy-start(bf16[160,1152]{1,0:T(8,128)(2,1)} %raw.3) | copy-start | bytes 1105924
  12.5 5.7 %copy-start.1 = (bf16[160,1152]{1,0:T(8,128)(2,1)S(1)}, bf16[160,1152]{1,0:T(8,128)(2,1)}, u32[]{:S(2)}) copy-start(bf16[160,1152]{1,0:T(8,128)(2,1)} %raw.2) | copy-start | bytes 1105924
  12.9 9.3 %collective-permute-start.4 = (bf16[160,1152]{1,0:T(8,128)(2,1)S(1)}, bf16[160,1152]{1,0:T(8,128)(2,1)S(1)}, u32[]{:S(2)}, u32[]{:S(2)}) collective-permute-start(bf16[160,1152]{1,0:T(8,128)(2,1)S(1)} %get-tuple-element.21), channel_id=1, source_target_pairs={{0,2},{1,3},{2,4},{3,5},{4,6},{5,7},{6,0},{7,1},{8,14},{9,15},{10,... | collective-permute-start | bytes 1105928 | tf_op jit(solution)/shard_map/ppermute | solution.py:37
  14.4 9.0 %collective-permute-start.5 = (bf16[160,1152]{1,0:T(8,128)(2,1)S(1)}, bf16[160,1152]{1,0:T(8,128)(2,1)S(1)}, u32[]{:S(2)}, u32[]{:S(2)}) collective-permute-start(bf16[160,1152]{1,0:T(8,128)(2,1)S(1)} %copy-done), channel_id=1, source_target_pairs={{0,8},{8,16},{16,24},{24,32},{32,40},{40,48},{48,56},{56,64},{64,7... | collective-permute-start | bytes 1105928 | tf_op jit(solution)/shard_map/ppermute | solution.py:18
  14.4 20.5 %collective-permute-start.7 = (bf16[320,1152]{1,0:T(8,128)(2,1)S(1)}, bf16[320,1152]{1,0:T(8,128)(2,1)S(1)}, u32[]{:S(2)}, u32[]{:S(2)}) collective-permute-start(bf16[320,1152]{1,0:T(8,128)(2,1)S(1)} %get-tuple-element.22.pair), channel_id=1, source_target_pairs={{0,120},{8,0},{16,8},{24,16},{32,24},{40,32},{48,40},{56,48},{64,5... | collective-permute-start | bytes 2211848 | tf_op jit(solution)/shard_map/ppermute | solution.py:18
  18.3 9.1 %collective-permute-start.1 = (bf16[160,1152]{1,0:T(8,128)(2,1)S(1)}, bf16[160,1152]{1,0:T(8,128)(2,1)S(1)}, u32[]{:S(2)}, u32[]{:S(2)}) collective-permute-start(bf16[160,1152]{1,0:T(8,128)(2,1)S(1)} %collective-permute-done.part_raw), channel_id=1, source_target_pairs={{0,8},{8,16},{16,24},{24,32},{32,40},{40,48},{48,56},{56,64},{64,7... | collective-permute-start | bytes 1105928 | tf_op jit(solution)/shard_map/ppermute | solution.py:18
  18.3 15.7 %collective-permute-start.6 = (bf16[160,1152]{1,0:T(8,128)(2,1)S(1)}, bf16[160,1152]{1,0:T(8,128)(2,1)S(1)}, u32[]{:S(2)}, u32[]{:S(2)}) collective-permute-start(bf16[160,1152]{1,0:T(8,128)(2,1)S(1)} %copy-done.1), channel_id=1, source_target_pairs={{0,120},{8,0},{16,8},{24,16},{32,24},{40,32},{48,40},{56,48},{64,5... | collective-permute-start | bytes 1105928 | tf_op jit(solution)/shard_map/ppermute | solution.py:18
  22.1 14.6 %collective-permute-start.11 = (bf16[160,1152]{1,0:T(8,128)(2,1)S(1)}, bf16[160,1152]{1,0:T(8,128)(2,1)S(1)}, u32[]{:S(2)}, u32[]{:S(2)}) collective-permute-start(bf16[160,1152]{1,0:T(8,128)(2,1)S(1)} %collective-permute-done.4.x2), channel_id=1, source_target_pairs={{0,120},{8,0},{16,8},{24,16},{32,24},{40,32},{48,40},{56,48},{64,5... | collective-permute-start | bytes 1105928 | tf_op jit(solution)/shard_map/ppermute | solution.py:18
  30.0 13.1 %collective-permute-start.10 = (bf16[160,1152]{1,0:T(8,128)(2,1)S(1)}, bf16[160,1152]{1,0:T(8,128)(2,1)S(1)}, u32[]{:S(2)}, u32[]{:S(2)}) collective-permute-start(bf16[160,1152]{1,0:T(8,128)(2,1)S(1)} %get-tuple-element.32), channel_id=1, source_target_pairs={{0,4},{1,5},{2,6},{3,7},{4,0},{5,1},{6,2},{7,3},{8,12},{9,13},{10,... | collective-permute-start | bytes 1105928 | tf_op jit(solution)/shard_map/ppermute | solution.py:27
  32.9 13.6 %collective-permute-start.8 = (bf16[160,1152]{1,0:T(8,128)(2,1)S(1)}, bf16[160,1152]{1,0:T(8,128)(2,1)S(1)}, u32[]{:S(2)}, u32[]{:S(2)}) collective-permute-start(bf16[160,1152]{1,0:T(8,128)(2,1)S(1)} %get-tuple-element.30), channel_id=1, source_target_pairs={{0,6},{1,7},{2,0},{3,1},{4,2},{5,3},{6,4},{7,5},{8,14},{9,15},{10,... | collective-permute-start | bytes 1105928 | tf_op jit(solution)/shard_map/ppermute | solution.py:27
  33.9 13.1 %collective-permute-start.9 = (bf16[160,1152]{1,0:T(8,128)(2,1)S(1)}, bf16[160,1152]{1,0:T(8,128)(2,1)S(1)}, u32[]{:S(2)}, u32[]{:S(2)}) collective-permute-start(bf16[160,1152]{1,0:T(8,128)(2,1)S(1)} %get-tuple-element.31), channel_id=1, source_target_pairs={{0,2},{1,3},{2,4},{3,5},{4,6},{5,7},{6,0},{7,1},{8,10},{9,11},{10,... | collective-permute-start | bytes 1105928 | tf_op jit(solution)/shard_map/ppermute | solution.py:27
  37.9 10.9 %collective-permute-start.12 = (bf16[160,1152]{1,0:T(8,128)(2,1)S(1)}, bf16[160,1152]{1,0:T(8,128)(2,1)S(1)}, u32[]{:S(2)}, u32[]{:S(2)}) collective-permute-start(bf16[160,1152]{1,0:T(8,128)(2,1)S(1)} %get-tuple-element.39), channel_id=1, source_target_pairs={{0,1},{1,0},{2,3},{3,2},{4,5},{5,4},{6,7},{7,6},{8,9},{9,8},{10,11... | collective-permute-start | bytes 1105928 | tf_op jit(solution)/shard_map/ppermute | solution.py:46

commit v3 on v2

v3 whole, which is shorter than its diff:
```python
import jax
import jax.numpy as jnp
from jax import lax
from jax.experimental import pallas as pl
from jax.experimental.pallas import tpu as pltpu
from jax.sharding import PartitionSpec as P

VMEM = pltpu.VMEM
LIMIT = 40 * 1024 * 1024
BLK_X = 4
BLK_Z = 2
BF16 = jnp.bfloat16
F32 = jnp.float32


def shift_prev(value, steps):
    count = lax.axis_size("outer")
    return lax.ppermute(value, "outer", [(s, (s + steps) % count) for s in range(count)])


def shift_x(value, steps):
    pairs = [
        (x * BLK_Z + z, (x + steps) % BLK_X * BLK_Z + z)
        for x in range(BLK_X)
        for z in range(BLK_Z)
    ]
    return lax.ppermute(value, "blk", pairs)


def shift_around(value, sign):
    outer, blk = lax.axis_size("outer"), lax.axis_size("blk")
    pairs = []
    for s in range(outer):
        for b in range(blk):
            x = (b // BLK_Z + sign * (1 - s % 2 * 2)) % BLK_X
            pairs.append((s * blk + b, s * blk + x * BLK_Z + b % BLK_Z))
    return lax.ppermute(value, ("outer", "blk"), pairs)


def swap_z(value):
    pairs = [
        (x * BLK_Z + z, x * BLK_Z + (BLK_Z - 1 - z))
        for x in range(BLK_X)
        for z in range(BLK_Z)
    ]
    return lax.ppermute(value, "blk", pairs)


def call(body, name, outs, flops, operands, scratch=(), smem=0, aliases=None):
    specs = [pl.BlockSpec(memory_space=pltpu.SMEM)] * smem
    specs += [pl.BlockSpec(memory_space=VMEM)] * (len(operands) - smem)
    size = sum(v.size * v.dtype.itemsize for v in operands)
    return pl.pallas_call(
        body,
        out_shape=outs,
        in_specs=specs,
        out_specs=[pl.BlockSpec(memory_space=VMEM)] * len(outs),
        scratch_shapes=list(scratch),
        input_output_aliases=aliases or {},
        compiler_params=pltpu.CompilerParams(vmem_limit_bytes=LIMIT),
        cost_estimate=pl.CostEstimate(flops=flops, bytes_accessed=0, transcendentals=0),
        name=name,
    )(*operands)


def normalized(ref):
    values = ref[...].astype(F32)
    inverse = 1.0 / jnp.sqrt(jnp.sum(values * values, axis=-1, keepdims=True) + 1e-06)
    return (values * inverse).astype(BF16)


def scores(left, right):
    return lax.dot_general(left, right, (((1,), (1,)), ((), ())), preferred_element_type=F32)


def sums(left, right):
    return lax.dot_general(left, right, (((0,), (0,)), ((), ())), preferred_element_type=F32)


def near_units_kernel(core, temp, bias, x1_raw, x3_raw, pair, sent):
    rows = sent.shape[0]
    pair[:rows, :] = normalized(x1_raw)
    pair[rows:, :] = normalized(x3_raw)

    @pl.when(core[0] == 0)
    def _():
        sent[...] = pair[:rows, :]

    @pl.when(core[0] != 0)
    def _():
        sent[...] = pair[rows:, :]


def unit_kernel(raw, out):
    out[...] = normalized(raw)


def early_kernel(temp, bias, images, texts, part, p0_raw, pair, img, txt, sig):
    rows = images.shape[0]
    img[:rows, :] = normalized(images)
    img[rows : 3 * rows, :] = pair[...]
    txt[:rows, :] = normalized(texts)
    txt[rows : 2 * rows, :] = part[...]
    txt[2 * rows : 3 * rows, :] = normalized(p0_raw)
    early = 3 * rows
    value = jax.nn.sigmoid(temp[0] * scores(img[:early, :], txt[:early, :]) + bias[0])
    row = lax.broadcasted_iota(jnp.int32, value.shape, 0)
    col = lax.broadcasted_iota(jnp.int32, value.shape, 1)
    same = jnp.logical_and(row == col, row < rows)
    sig[:early, :early] = (value - same.astype(F32)).astype(BF16)


def far_kernel(temp, bias, x2, txt, img_in, sig_in, img, sig, acc):
    rows = x2.shape[0]
    early = 3 * rows
    img[early:, :] = x2[...]
    value = jax.nn.sigmoid(temp[0] * scores(x2[...], txt[:early, :]) + bias[0])
    sig[early:, :early] = value.astype(BF16)
    acc[...] = jnp.dot(
        sig[rows:, :early], txt[:early, :], preferred_element_type=F32
    )


def late_kernel(
    temp, bias, p1, acc, img, txt_in, sig_in, txt, sig, d1, d3, d2
):
    rows = p1.shape[0]
    early = 3 * rows
    txt[early:, :] = p1[...]
    value = jax.nn.sigmoid(temp[0] * scores(img[...], p1[...]) + bias[0]).astype(BF16)
    sig[:, early:] = value
    rest = jnp.dot(value[rows:, :], p1[...], preferred_element_type=F32)
    total = temp[0] * (acc[...] + rest)
    for k, out in enumerate((d1, d3, d2)):
        out[...] = total[k * rows : (k + 1) * rows, :].astype(BF16)


def middle_kernel(
    temp, bias, img, txt, sig, n0_raw, n_pair, d0, e_own, e_part, nxt, sig_next
):
    rows = d0.shape[0]
    d0[...] = temp[0] * jnp.dot(sig[:rows, :], txt[...], preferred_element_type=F32)
    nxt[:rows, :] = normalized(n0_raw)
    nxt[rows:, :] = n_pair[...]
    value = scores(nxt[...], txt[: 2 * rows, :])
    sig_next[...] = jax.nn.sigmoid(temp[0] * value + bias[0]).astype(BF16)
    for k, out in enumerate((e_own, e_part)):
        mine = slice(k * rows, (k + 1) * rows)
        out[...] = temp[0] * (sums(sig[:, mine], img[...]) + sums(sig_next[:, mine], nxt[...]))


def part_kernel(temp, bias, n2, txt, e_part, sig_next, to_part):
    rows = n2.shape[0]
    value = scores(n2[...], txt[: 2 * rows, :])
    sig_next[...] = jax.nn.sigmoid(temp[0] * value + bias[0]).astype(BF16)
    total = e_part[...] + temp[0] * sums(sig_next[:, rows:], n2[...])
    to_part[...] = total.astype(BF16)


def own_kernel(temp, e_own, n2, sig_next, out):
    rows = out.shape[0]
    out[...] = e_own[...] + temp[0] * sums(sig_next[:, :rows], n2[...])


def finish_kernel(raw, own, *rest):
    out = rest[-1]
    values = raw[...].astype(F32)
    total = own[...]
    for ref in rest[:-1]:
        total = total + ref[...].astype(F32)
    inverse = 1.0 / jnp.sqrt(jnp.sum(values * values, axis=-1, keepdims=True) + 1e-06)
    inner = jnp.sum(values * total, axis=-1, keepdims=True) * inverse
    out[...] = (total * inverse - values * (inner * inverse * inverse)).astype(out.dtype)


def local(images, texts, temp, bias):
    shape = images.shape
    rows, width = shape
    many = 4 * rows
    tile = 2 * rows * rows * width
    f32 = jax.ShapeDtypeStruct(shape, F32)
    b16 = jax.ShapeDtypeStruct(shape, BF16)
    stack = jax.ShapeDtypeStruct((many, width), BF16)
    sigs = jax.ShapeDtypeStruct((many, many), BF16)
    halves = jax.ShapeDtypeStruct((rows, 2 * rows), BF16)
    wide = jax.ShapeDtypeStruct((2 * rows, width), BF16)
    triple = jax.ShapeDtypeStruct((3 * rows, width), F32)
    core = (lax.axis_index("outer") % 2).astype(jnp.int32).reshape(1)

    part_raw = swap_z(texts)
    x1_raw = shift_x(images, 1)
    x3_raw = shift_x(images, -1)
    later, x1_raw = lax.optimization_barrier((texts, x1_raw))
    p0_raw = shift_prev(later, 1)
    (part,) = call(unit_kernel, "unit_part", [b16], 1000000000, (part_raw,))
    p1 = shift_prev(part, 1)
    later, x3_raw = lax.optimization_barrier((images, x3_raw))
    n0_raw = shift_prev(later, -1)
    pair, sent = call(
        near_units_kernel, "units_near", [wide, b16], 1000000000, (core, temp, bias, x1_raw, x3_raw), smem=3
    )
    x2 = shift_around(sent, 1)
    n_pair = shift_prev(pair, -1)
    n2 = shift_prev(x2, -1)

    img, txt, sig = call(
        early_kernel, "early_pairs", [stack, stack, sigs], 3000000000,
        (temp, bias, images, texts, part, p0_raw, pair), smem=2,
    )
    img, sig, acc = call(
        far_kernel, "far_pairs", [stack, sigs, triple], 1000000000,
        (temp, bias, x2, txt, img, sig), smem=2, aliases={4: 0, 5: 1},
    )
    txt, sig, d1, d3, d2 = call(
        late_kernel, "late_pairs", [stack, sigs] + [b16] * 3, 1000000000,
        (temp, bias, p1, acc, img, txt, sig), smem=2, aliases={5: 0, 6: 1},
    )
    r1 = shift_x(d1, -1)
    r3 = shift_x(d3, 1)
    r2 = shift_x(d2, 2)
    d0, e_own, e_part = call(
        middle_kernel, "middle_sums", [f32] * 3, 1000000000,
        (temp, bias, img, txt, sig, n0_raw, n_pair),
        [VMEM((3 * rows, width), BF16), VMEM((3 * rows, 2 * rows), BF16)], smem=2,
    )
    sig_next, to_part = call(
        part_kernel, "part_sums", [halves, b16], 1000000000,
        (temp, bias, n2, txt, e_part), smem=2,
    )
    from_part = swap_z(to_part)
    (e_own,) = call(own_kernel, "own_sums", [f32], 1000000000, (temp, e_own, n2, sig_next), smem=1)
    (grad_images,) = call(
        finish_kernel, "finish_images", [b16], 1000000000, (images, d0, r1, r3, r2)
    )
    (grad_texts,) = call(
        finish_kernel, "finish_texts", [b16], 1000000000, (texts, e_own, from_part)
    )
    return (grad_images, grad_texts)


def solution(mesh):
    spec = P(("outer", "blk"), None)
    return jax.shard_map(
        local,
        mesh=mesh,
        in_specs=(spec, spec, P(), P()),
        out_specs=(spec, spec),
        check_vma=False,
    )
```

time: 50.4 us -> 50 us (level)
    ppermute x2, waiting for transfers between devices: 0.01 us -> 0.9 us  [swap_z(): return lax.ppermute(value, 'blk', pairs)]
    ppermute x5, waiting for transfers between devices: 3.4 us -> 2.55 us  [shift_prev(): lax.ppermute(value, 'outer', [(s, (s + steps) % count) for s in range(cou...]
    pallas_call x8 -> x10, Pallas kernels: 9.88 us -> 10.2 us  [call(): pl.pallas_call(body, out_shape=outs, in_specs=specs, out_specs=[pl.BlockS...]
  transfers between devices with their start and end apart: 13 -> 13, of which waited for: 7 -> 8; matrix products, arithmetic and copies ran while one was open for 0% -> 0% of each run, Pallas kernels for 18% -> 18%
where the time goes in v3:
time: 50 us; the launch traced here: 49.9 us
  starting transfers between devices  25.8 us (52%)
  waiting for transfers between devices  11.8 us (24%)
  Pallas kernels  10.2 us (20%)
  between operations  2.02 us (4%)
    pallas_call x10, Pallas kernels, call(): pl.pallas_call(body, out_shape=outs, in_specs=specs, out_specs=[pl.BlockS...  10.2 us
    ppermute x5, waiting for transfers between devices, shift_x(): return lax.ppermute(value, 'blk', pairs)  8.37 us
    ppermute x5, starting transfers between devices, shift_x(): return lax.ppermute(value, 'blk', pairs)  8.21 us
    ppermute x5, starting transfers between devices, shift_prev(): lax.ppermute(value, 'outer', [(s, (s + steps) % count) for s in range(cou...  8.05 us
    ppermute x2, starting transfers between devices, swap_z(): return lax.ppermute(value, 'blk', pairs)  8.02 us
    ppermute x5, waiting for transfers between devices, shift_prev(): lax.ppermute(value, 'outer', [(s, (s + steps) % count) for s in range(cou...  2.55 us
    ppermute x1, starting transfers between devices, shift_around(): return lax.ppermute(value, ('outer', 'blk'), pairs)  1.56 us
  transfers between devices with their start and end apart: 13, of which 8 were waited for; matrix products, arithmetic and copies ran while one was open for 0% of the time, Pallas kernels for 18%

profile of v3, /device:TPU:0, one launch (start us, length us, event | category | flops | bytes accessed | tf_op | source)
XLA Modules:
  0.0 49.9 jit_solution(17324579646887852325)
XLA Ops:
  0.6 1.6 %collective-permute-start = (bf16[160,1152]{1,0:T(8,128)(2,1)}, bf16[160,1152]{1,0:T(8,128)(2,1)S(1)}, u32[]{:S(2)}, u32[]{:S(2)}) collective-permute-start(bf16[160,1152]{1,0:T(8,128)(2,1)} %raw.2), channel_id=1, source_target_pairs={{0,2},{1,3},{2,4},{3,5},{4,6},{5,7},{6,0},{7,1},{8,10},{9,11},{10,... | collective-permute-start | bytes 1105928 | tf_op jit(solution)/shard_map/ppermute | solution.py:27
  2.3 1.7 %collective-permute-start.1 = (bf16[160,1152]{1,0:T(8,128)(2,1)}, bf16[160,1152]{1,0:T(8,128)(2,1)S(1)}, u32[]{:S(2)}, u32[]{:S(2)}) collective-permute-start(bf16[160,1152]{1,0:T(8,128)(2,1)} %raw.2), channel_id=1, source_target_pairs={{0,6},{1,7},{2,0},{3,1},{4,2},{5,3},{6,4},{7,5},{8,14},{9,15},{10,... | collective-permute-start | bytes 1105928 | tf_op jit(solution)/shard_map/ppermute | solution.py:27
  3.9 4.0 %collective-permute-start.3 = (bf16[160,1152]{1,0:T(8,128)(2,1)}, bf16[160,1152]{1,0:T(8,128)(2,1)S(1)}, u32[]{:S(2)}, u32[]{:S(2)}) collective-permute-start(bf16[160,1152]{1,0:T(8,128)(2,1)} %raw.3), channel_id=1, source_target_pairs={{0,1},{1,0},{2,3},{3,2},{4,5},{5,4},{6,7},{7,6},{8,9},{9,8},{10,11... | collective-permute-start | bytes 1105928 | tf_op jit(solution)/shard_map/ppermute | solution.py:46
  9.2 3.1 %collective-permute-done.x1_raw = bf16[160,1152]{1,0:T(8,128)(2,1)S(1)} collective-permute-done((bf16[160,1152]{1,0:T(8,128)(2,1)}, bf16[160,1152]{1,0:T(8,128)(2,1)S(1)}, u32[]{:S(2)}, u32[]{:S(2)}) %collective-permute-start) | collective-permute-done | bytes 368672 | tf_op jit(solution)/shard_map/ppermute | solution.py:27
  12.8 1.6 %collective-permute-start.2 = (bf16[160,1152]{1,0:T(8,128)(2,1)S(1)}, bf16[160,1152]{1,0:T(8,128)(2,1)S(1)}, u32[]{:S(2)}, u32[]{:S(2)}) collective-permute-start(bf16[160,1152]{1,0:T(8,128)(2,1)S(1)} %get-tuple-element.26), channel_id=1, source_target_pairs={{0,2},{1,3},{2,4},{3,5},{4,6},{5,7},{6,0},{7,1},{8,14},{9,15},{10,... | collective-permute-start | bytes 1105928 | tf_op jit(solution)/shard_map/ppermute | solution.py:37
  14.4 3.9 %collective-permute-start.7 = (bf16[320,1152]{1,0:T(8,128)(2,1)S(1)}, bf16[320,1152]{1,0:T(8,128)(2,1)S(1)}, u32[]{:S(2)}, u32[]{:S(2)}) collective-permute-start(bf16[320,1152]{1,0:T(8,128)(2,1)S(1)} %get-tuple-element.28.pair), channel_id=1, source_target_pairs={{0,120},{8,0},{16,8},{24,16},{32,24},{40,32},{48,40},{56,48},{64,5... | collective-permute-start | bytes 2211848 | tf_op jit(solution)/shard_map/ppermute | solution.py:18
  18.6 3.8 %collective-permute-start.6 = (bf16[160,1152]{1,0:T(8,128)(2,1)S(1)}, bf16[160,1152]{1,0:T(8,128)(2,1)S(1)}, u32[]{:S(2)}, u32[]{:S(2)}) collective-permute-start(bf16[160,1152]{1,0:T(8,128)(2,1)S(1)} %copy-done), channel_id=1, source_target_pairs={{0,120},{8,0},{16,8},{24,16},{32,24},{40,32},{48,40},{56,48},{64,5... | collective-permute-start | bytes 1105928 | tf_op jit(solution)/shard_map/ppermute | solution.py:18
  22.7 0.8 %collective-permute-done.4.p0_raw = bf16[160,1152]{1,0:T(8,128)(2,1)S(1)} collective-permute-done((bf16[160,1152]{1,0:T(8,128)(2,1)S(1)}, bf16[160,1152]{1,0:T(8,128)(2,1)S(1)}, u32[]{:S(2)}, u32[]{:S(2)}) %collective-permute-start.4) | collective-permute-done | bytes 368672 | tf_op jit(solution)/shard_map/ppermute | solution.py:18
  23.5 1.2 %early_pairs.1 = (bf16[640,1152]{1,0:T(8,128)(2,1)S(1)}, bf16[640,1152]{1,0:T(8,128)(2,1)S(1)}, bf16[640,640]{1,0:T(8,128)(2,1)S(1)}) custom-call(f32[1]{0:T(128)S(6)} %copy.14.temp, f32[1]{0:T(128)S(6)} %copy.15.bias, bf16[160,1152]{1,0:T(8,128)(2,1)S(1)} %copy-done, bf16[160,1152]{1,0:T(8,128)(2,1)S(1)} %copy-done.1, bf16[160,1152]{1,0:T(8,128)(2,1)S(1)} %unit_part.1.part, ...), custom_call_target="tpu_custom_call" | custom-call | flops 3000000000 | tf_op jit(solution)/shard_map/early_pairs/pallas_call | solution.py:53
  24.6 1.2 %far_pairs.1 = (bf16[640,1152]{1,0:T(8,128)(2,1)S(1)}, bf16[640,640]{1,0:T(8,128)(2,1)S(1)}, f32[480,1152]{1,0:T(8,128)S(1)}) custom-call(f32[1]{0:T(128)S(6)} %copy.14.temp, f32[1]{0:T(128)S(6)} %copy.15.bias, bf16[160,1152]{1,0:T(8,128)(2,1)S(1)} %collective-permute-done.2.x2, ...), custom_call_target="tpu_custom_call", output_to_operand_aliasing={{0}: (4, {}), {1}: (5, {})} | custom-call | flops 1000000000 | tf_op jit(solution)/shard_map/far_pairs/pallas_call | solution.py:53
  25.8 1.8 %collective-permute-done.5.p1 = bf16[160,1152]{1,0:T(8,128)(2,1)S(1)} collective-permute-done((bf16[160,1152]{1,0:T(8,128)(2,1)S(1)}, bf16[160,1152]{1,0:T(8,128)(2,1)S(1)}, u32[]{:S(2)}, u32[]{:S(2)}) %collective-permute-start.5) | collective-permute-done | bytes 368672 | tf_op jit(solution)/shard_map/ppermute | solution.py:18
  27.6 1.5 %late_pairs.1 = (bf16[640,1152]{1,0:T(8,128)(2,1)S(1)}, bf16[640,640]{1,0:T(8,128)(2,1)S(1)}, bf16[160,1152]{1,0:T(8,128)(2,1)S(1)}, bf16[160,1152]{1,0:T(8,128)(2,1)S(1)}, bf16[160,1152]{1,0:T(8,128)(2,1)S(1)}) custom-call(f32[1]{0:T(128)S(6)} %copy.14.temp, f32[1]{0:T(128)S(6)} %copy.15.bias, ...), custom_call_target="tpu_custom_call", output_to_operand_aliasing={{0}: (5, {}), {1}: (6, {})} | custom-call | flops 1000000000 | tf_op jit(solution)/shard_map/late_pairs/pallas_call | solution.py:53
  29.1 2.9 %collective-permute-start.10 = (bf16[160,1152]{1,0:T(8,128)(2,1)S(1)}, bf16[160,1152]{1,0:T(8,128)(2,1)S(1)}, u32[]{:S(2)}, u32[]{:S(2)}) collective-permute-start(bf16[160,1152]{1,0:T(8,128)(2,1)S(1)} %get-tuple-element.41), channel_id=1, source_target_pairs={{0,4},{1,5},{2,6},{3,7},{4,0},{5,1},{6,2},{7,3},{8,12},{9,13},{10,... | collective-permute-start | bytes 1105928 | tf_op jit(solution)/shard_map/ppermute | solution.py:27
  32.0 1.1 %collective-permute-start.8 = (bf16[160,1152]{1,0:T(8,128)(2,1)S(1)}, bf16[160,1152]{1,0:T(8,128)(2,1)S(1)}, u32[]{:S(2)}, u32[]{:S(2)}) collective-permute-start(bf16[160,1152]{1,0:T(8,128)(2,1)S(1)} %get-tuple-element.39), channel_id=1, source_target_pairs={{0,6},{1,7},{2,0},{3,1},{4,2},{5,3},{6,4},{7,5},{8,14},{9,15},{10,... | collective-permute-start | bytes 1105928 | tf_op jit(solution)/shard_map/ppermute | solution.py:27
  33.1 1.0 %collective-permute-start.9 = (bf16[160,1152]{1,0:T(8,128)(2,1)S(1)}, bf16[160,1152]{1,0:T(8,128)(2,1)S(1)}, u32[]{:S(2)}, u32[]{:S(2)}) collective-permute-start(bf16[160,1152]{1,0:T(8,128)(2,1)S(1)} %get-tuple-element.40), channel_id=1, source_target_pairs={{0,2},{1,3},{2,4},{3,5},{4,6},{5,7},{6,0},{7,1},{8,10},{9,11},{10,... | collective-permute-start | bytes 1105928 | tf_op jit(solution)/shard_map/ppermute | solution.py:27
  34.0 2.4 %middle_sums.1 = (f32[160,1152]{1,0:T(8,128)S(1)}, f32[160,1152]{1,0:T(8,128)S(1)}, f32[160,1152]{1,0:T(8,128)S(1)}) custom-call(f32[1]{0:T(128)S(6)} %copy.14.temp, f32[1]{0:T(128)S(6)} %copy.15.bias, bf16[640,1152]{1,0:T(8,128)(2,1)S(1)} %get-tuple-element.32.img, bf16[640,1152]{1,0:T(8,128)(2,1)S(1)} %get-tuple-element.35.txt, ...), custom_call_target="tpu_custom_call" | custom-call | flops 1000000000 | tf_op jit(solution)/shard_map/middle_sums/pallas_call | solution.py:53
  36.5 0.9 %part_sums.1 = (bf16[160,320]{1,0:T(8,128)(2,1)S(1)}, bf16[160,1152]{1,0:T(8,128)(2,1)S(1)}) custom-call(f32[1]{0:T(128)S(6)} %copy.14.temp, f32[1]{0:T(128)S(6)} %copy.15.bias, bf16[160,1152]{1,0:T(8,128)(2,1)S(1)} %collective-permute-done.11.n2, bf16[640,1152]{1,0:T(8,128)(2,1)S(1)} %get-tuple-element.35.txt, f32[160,1152]{1,0:T(8,128)S(1)} %get-tuple-element.43.e_part), custom_call_target="tpu_custom_call" | custom-call | flops 1000000000 | tf_op jit(solution)/shard_map/part_sums/pallas_call | solution.py:53
  37.4 4.1 %collective-permute-start.12 = (bf16[160,1152]{1,0:T(8,128)(2,1)S(1)}, bf16[160,1152]{1,0:T(8,128)(2,1)S(1)}, u32[]{:S(2)}, u32[]{:S(2)}) collective-permute-start(bf16[160,1152]{1,0:T(8,128)(2,1)S(1)} %get-tuple-element.45), channel_id=1, source_target_pairs={{0,1},{1,0},{2,3},{3,2},{4,5},{5,4},{6,7},{7,6},{8,9},{9,8},{10,11... | collective-permute-start | bytes 1105928 | tf_op jit(solution)/shard_map/ppermute | solution.py:46
  41.8 0.5 collective-permute-done.10.rest_2_
  42.2 3.9 %collective-permute-done.8.rest_0_ = bf16[160,1152]{1,0:T(8,128)(2,1)S(1)} collective-permute-done((bf16[160,1152]{1,0:T(8,128)(2,1)S(1)}, bf16[160,1152]{1,0:T(8,128)(2,1)S(1)}, u32[]{:S(2)}, u32[]{:S(2)}) %collective-permute-start.8) | collective-permute-done | bytes 368672 | tf_op jit(solution)/shard_map/ppermute | solution.py:27
  46.1 0.7 %collective-permute-done.9.rest_1_ = bf16[160,1152]{1,0:T(8,128)(2,1)S(1)} collective-permute-done((bf16[160,1152]{1,0:T(8,128)(2,1)S(1)}, bf16[160,1152]{1,0:T(8,128)(2,1)S(1)}, u32[]{:S(2)}, u32[]{:S(2)}) %collective-permute-start.9) | collective-permute-done | bytes 368672 | tf_op jit(solution)/shard_map/ppermute | solution.py:27
  46.8 1.1 %finish_images.1 = bf16[160,1152]{1,0:T(8,128)(2,1)} custom-call(bf16[160,1152]{1,0:T(8,128)(2,1)S(1)} %copy-done, f32[160,1152]{1,0:T(8,128)S(1)} %get-tuple-element.38.own, bf16[160,1152]{1,0:T(8,128)(2,1)S(1)} %collective-permute-done.8.rest_0_, bf16[160,1152]{1,0:T(8,128)(2,1)S(1)} %collective-permute-done.9.rest_1_, ...), custom_call_target="tpu_custom_call" | custom-call | flops 1000000000 | tf_op jit(solution)/shard_map/finish_images/pallas_call | solution.py:53
  48.0 0.9 %collective-permute-done.12.rest_0_ = bf16[160,1152]{1,0:T(8,128)(2,1)S(1)} collective-permute-done((bf16[160,1152]{1,0:T(8,128)(2,1)S(1)}, bf16[160,1152]{1,0:T(8,128)(2,1)S(1)}, u32[]{:S(2)}, u32[]{:S(2)}) %collective-permute-start.12) | collective-permute-done | bytes 368672 | tf_op jit(solution)/shard_map/ppermute | solution.py:46
  48.8 1.1 %finish_texts.1 = bf16[160,1152]{1,0:T(8,128)(2,1)} custom-call(bf16[160,1152]{1,0:T(8,128)(2,1)S(1)} %copy-done.1, f32[160,1152]{1,0:T(8,128)S(1)} %own_sums.1.own, bf16[160,1152]{1,0:T(8,128)(2,1)S(1)} %collective-permute-done.12.rest_0_), custom_call_target="tpu_custom_call" | custom-call | flops 1000000000 | tf_op jit(solution)/shard_map/finish_texts/pallas_call | solution.py:53
  (16 shorter events, 1.3 us)
Async XLA Ops:
  0.6 11.7 %collective-permute-start = (bf16[160,1152]{1,0:T(8,128)(2,1)}, bf16[160,1152]{1,0:T(8,128)(2,1)S(1)}, u32[]{:S(2)}, u32[]{:S(2)}) collective-permute-start(bf16[160,1152]{1,0:T(8,128)(2,1)} %raw.2), channel_id=1, source_target_pairs={{0,2},{1,3},{2,4},{3,5},{4,6},{5,7},{6,0},{7,1},{8,10},{9,11},{10,... | collective-permute-start | bytes 1105928 | tf_op jit(solution)/shard_map/ppermute | solution.py:27
  2.3 10.3 %collective-permute-start.1 = (bf16[160,1152]{1,0:T(8,128)(2,1)}, bf16[160,1152]{1,0:T(8,128)(2,1)S(1)}, u32[]{:S(2)}, u32[]{:S(2)}) collective-permute-start(bf16[160,1152]{1,0:T(8,128)(2,1)} %raw.2), channel_id=1, source_target_pairs={{0,6},{1,7},{2,0},{3,1},{4,2},{5,3},{6,4},{7,5},{8,14},{9,15},{10,... | collective-permute-start | bytes 1105928 | tf_op jit(solution)/shard_map/ppermute | solution.py:27
  3.9 14.3 %collective-permute-start.3 = (bf16[160,1152]{1,0:T(8,128)(2,1)}, bf16[160,1152]{1,0:T(8,128)(2,1)S(1)}, u32[]{:S(2)}, u32[]{:S(2)}) collective-permute-start(bf16[160,1152]{1,0:T(8,128)(2,1)} %raw.3), channel_id=1, source_target_pairs={{0,1},{1,0},{2,3},{3,2},{4,5},{5,4},{6,7},{7,6},{8,9},{9,8},{10,11... | collective-permute-start | bytes 1105928 | tf_op jit(solution)/shard_map/ppermute | solution.py:46
  12.5 1.9 %copy-start.1 = (bf16[160,1152]{1,0:T(8,128)(2,1)S(1)}, bf16[160,1152]{1,0:T(8,128)(2,1)}, u32[]{:S(2)}) copy-start(bf16[160,1152]{1,0:T(8,128)(2,1)} %raw.3) | copy-start | bytes 1105924
  12.8 9.5 %collective-permute-start.2 = (bf16[160,1152]{1,0:T(8,128)(2,1)S(1)}, bf16[160,1152]{1,0:T(8,128)(2,1)S(1)}, u32[]{:S(2)}, u32[]{:S(2)}) collective-permute-start(bf16[160,1152]{1,0:T(8,128)(2,1)S(1)} %get-tuple-element.26), channel_id=1, source_target_pairs={{0,2},{1,3},{2,4},{3,5},{4,6},{5,7},{6,0},{7,1},{8,14},{9,15},{10,... | collective-permute-start | bytes 1105928 | tf_op jit(solution)/shard_map/ppermute | solution.py:37
  14.4 9.0 %collective-permute-start.4 = (bf16[160,1152]{1,0:T(8,128)(2,1)S(1)}, bf16[160,1152]{1,0:T(8,128)(2,1)S(1)}, u32[]{:S(2)}, u32[]{:S(2)}) collective-permute-start(bf16[160,1152]{1,0:T(8,128)(2,1)S(1)} %copy-done.1), channel_id=1, source_target_pairs={{0,8},{8,16},{16,24},{24,32},{32,40},{40,48},{48,56},{56,64},{64,7... | collective-permute-start | bytes 1105928 | tf_op jit(solution)/shard_map/ppermute | solution.py:18
  14.4 4.1 %copy-start = (bf16[160,1152]{1,0:T(8,128)(2,1)S(1)}, bf16[160,1152]{1,0:T(8,128)(2,1)}, u32[]{:S(2)}) copy-start(bf16[160,1152]{1,0:T(8,128)(2,1)} %raw.2) | copy-start | bytes 1105924
  14.4 19.6 %collective-permute-start.7 = (bf16[320,1152]{1,0:T(8,128)(2,1)S(1)}, bf16[320,1152]{1,0:T(8,128)(2,1)S(1)}, u32[]{:S(2)}, u32[]{:S(2)}) collective-permute-start(bf16[320,1152]{1,0:T(8,128)(2,1)S(1)} %get-tuple-element.28.pair), channel_id=1, source_target_pairs={{0,120},{8,0},{16,8},{24,16},{32,24},{40,32},{48,40},{56,48},{64,5... | collective-permute-start | bytes 2211848 | tf_op jit(solution)/shard_map/ppermute | solution.py:18
  18.5 9.1 %collective-permute-start.5 = (bf16[160,1152]{1,0:T(8,128)(2,1)S(1)}, bf16[160,1152]{1,0:T(8,128)(2,1)S(1)}, u32[]{:S(2)}, u32[]{:S(2)}) collective-permute-start(bf16[160,1152]{1,0:T(8,128)(2,1)S(1)} %unit_part.1.part), channel_id=1, source_target_pairs={{0,8},{8,16},{16,24},{24,32},{32,40},{40,48},{48,56},{56,64},{64,7... | collective-permute-start | bytes 1105928 | tf_op jit(solution)/shard_map/ppermute | solution.py:18
  18.6 14.5 %collective-permute-start.6 = (bf16[160,1152]{1,0:T(8,128)(2,1)S(1)}, bf16[160,1152]{1,0:T(8,128)(2,1)S(1)}, u32[]{:S(2)}, u32[]{:S(2)}) collective-permute-start(bf16[160,1152]{1,0:T(8,128)(2,1)S(1)} %copy-done), channel_id=1, source_target_pairs={{0,120},{8,0},{16,8},{24,16},{32,24},{40,32},{48,40},{56,48},{64,5... | collective-permute-start | bytes 1105928 | tf_op jit(solution)/shard_map/ppermute | solution.py:18
  22.4 14.1 %collective-permute-start.11 = (bf16[160,1152]{1,0:T(8,128)(2,1)S(1)}, bf16[160,1152]{1,0:T(8,128)(2,1)S(1)}, u32[]{:S(2)}, u32[]{:S(2)}) collective-permute-start(bf16[160,1152]{1,0:T(8,128)(2,1)S(1)} %collective-permute-done.2.x2), channel_id=1, source_target_pairs={{0,120},{8,0},{16,8},{24,16},{32,24},{40,32},{48,40},{56,48},{64,5... | collective-permute-start | bytes 1105928 | tf_op jit(solution)/shard_map/ppermute | solution.py:18
  29.1 13.1 %collective-permute-start.10 = (bf16[160,1152]{1,0:T(8,128)(2,1)S(1)}, bf16[160,1152]{1,0:T(8,128)(2,1)S(1)}, u32[]{:S(2)}, u32[]{:S(2)}) collective-permute-start(bf16[160,1152]{1,0:T(8,128)(2,1)S(1)} %get-tuple-element.41), channel_id=1, source_target_pairs={{0,4},{1,5},{2,6},{3,7},{4,0},{5,1},{6,2},{7,3},{8,12},{9,13},{10,... | collective-permute-start | bytes 1105928 | tf_op jit(solution)/shard_map/ppermute | solution.py:27
  32.0 14.1 %collective-permute-start.8 = (bf16[160,1152]{1,0:T(8,128)(2,1)S(1)}, bf16[160,1152]{1,0:T(8,128)(2,1)S(1)}, u32[]{:S(2)}, u32[]{:S(2)}) collective-permute-start(bf16[160,1152]{1,0:T(8,128)(2,1)S(1)} %get-tuple-element.39), channel_id=1, source_target_pairs={{0,6},{1,7},{2,0},{3,1},{4,2},{5,3},{6,4},{7,5},{8,14},{9,15},{10,... | collective-permute-start | bytes 1105928 | tf_op jit(solution)/shard_map/ppermute | solution.py:27
  33.1 13.7 %collective-permute-start.9 = (bf16[160,1152]{1,0:T(8,128)(2,1)S(1)}, bf16[160,1152]{1,0:T(8,128)(2,1)S(1)}, u32[]{:S(2)}, u32[]{:S(2)}) collective-permute-start(bf16[160,1152]{1,0:T(8,128)(2,1)S(1)} %get-tuple-element.40), channel_id=1, source_target_pairs={{0,2},{1,3},{2,4},{3,5},{4,6},{5,7},{6,0},{7,1},{8,10},{9,11},{10,... | collective-permute-start | bytes 1105928 | tf_op jit(solution)/shard_map/ppermute | solution.py:27
  37.4 11.4 %collective-permute-start.12 = (bf16[160,1152]{1,0:T(8,128)(2,1)S(1)}, bf16[160,1152]{1,0:T(8,128)(2,1)S(1)}, u32[]{:S(2)}, u32[]{:S(2)}) collective-permute-start(bf16[160,1152]{1,0:T(8,128)(2,1)S(1)} %get-tuple-element.45), channel_id=1, source_target_pairs={{0,1},{1,0},{2,3},{3,2},{4,5},{5,4},{6,7},{7,6},{8,9},{9,8},{10,11... | collective-permute-start | bytes 1105928 | tf_op jit(solution)/shard_map/ppermute | solution.py:46

commit v4 on v3

--- a/solution.py
+++ b/solution.py
@@ -9,6 +9,7 @@
 LIMIT = 40 * 1024 * 1024
 BLK_X = 4
 BLK_Z = 2
+CHUNKS = 5
 BF16 = jnp.bfloat16
 F32 = jnp.float32
 
@@ -49,7 +50,6 @@
 def call(body, name, outs, flops, operands, scratch=(), smem=0, aliases=None):
     specs = [pl.BlockSpec(memory_space=pltpu.SMEM)] * smem
     specs += [pl.BlockSpec(memory_space=VMEM)] * (len(operands) - smem)
-    size = sum(v.size * v.dtype.itemsize for v in operands)
     return pl.pallas_call(
         body,
         out_shape=outs,
@@ -163,14 +163,39 @@
 
 
 def finish_kernel(raw, own, *rest):
-    out = rest[-1]
-    values = raw[...].astype(F32)
-    total = own[...]
-    for ref in rest[:-1]:
-        total = total + ref[...].astype(F32)
-    inverse = 1.0 / jnp.sqrt(jnp.sum(values * values, axis=-1, keepdims=True) + 1e-06)
-    inner = jnp.sum(values * total, axis=-1, keepdims=True) * inverse
-    out[...] = (total * inverse - values * (inner * inverse * inverse)).astype(out.dtype)
+    *received, out, buffer, sems = rest
+    step = buffer.shape[0] // CHUNKS
+    copies = []
+    for k in range(CHUNKS):
+        mine = slice(k * step, (k + 1) * step)
+        values = raw[mine, :].astype(F32)
+        total = own[mine, :]
+        for ref in received:
+            total = total + ref[mine, :].astype(F32)
+        square = jnp.sum(values * values, axis=-1, keepdims=True)
+        inverse = 1.0 / jnp.sqrt(square + 1e-06)
+        inner = jnp.sum(values * total, axis=-1, keepdims=True) * inverse
+        grad = total * inverse - values * (inner * inverse * inverse)
+        buffer[mine, :] = grad.astype(out.dtype)
+        copy = pltpu.make_async_copy(buffer.at[mine, :], out.at[mine, :], sems.at[k])
+        copy.start()
+        copies.append(copy)
+    for copy in copies:
+        copy.wait()
+
+
+def finish(name, flops, operands):
+    raw = operands[0]
+    return pl.pallas_call(
+        finish_kernel,
+        out_shape=jax.ShapeDtypeStruct(raw.shape, BF16),
+        in_specs=[pl.BlockSpec(memory_space=VMEM)] * len(operands),
+        out_specs=pl.BlockSpec(memory_space=pl.ANY),
+        scratch_shapes=[VMEM(raw.shape, BF16), pltpu.SemaphoreType.DMA((CHUNKS,))],
+        compiler_params=pltpu.CompilerParams(vmem_limit_bytes=LIMIT),
+        cost_estimate=pl.CostEstimate(flops=flops, bytes_accessed=0, transcendentals=0),
+        name=name,
+    )(*operands)
 
 
 def local(images, texts, temp, bias):
@@ -229,12 +254,8 @@
     )
     from_part = swap_z(to_part)
     (e_own,) = call(own_kernel, "own_sums", [f32], 1000000000, (temp, e_own, n2, sig_next), smem=1)
-    (grad_images,) = call(
-        finish_kernel, "finish_images", [b16], 1000000000, (images, d0, r1, r3, r2)
-    )
-    (grad_texts,) = call(
-        finish_kernel, "finish_texts", [b16], 1000000000, (texts, e_own, from_part)
-    )
+    grad_images = finish("finish_images", 1000000000, (images, d0, r1, r3, r2))
+    grad_texts = finish("finish_texts", 1000000000, (texts, e_own, from_part))
     return (grad_images, grad_texts)
 
 

time: 50 us -> 50 us (level)
    pallas_call x10 -> x8, Pallas kernels: 10.2 us -> 8.01 us  [call(): pl.pallas_call(body, out_shape=outs, in_specs=specs, out_specs=[pl.BlockS...]
    pallas_call x0 -> x2, Pallas kernels: none -> 2.12 us  [finish(): pl.pallas_call(finish_kernel, out_shape=jax.ShapeDtypeStruct(raw.shape, B...]
where the time goes in v4:
time: 50 us; the launch traced here: 49.9 us
  starting transfers between devices  25.8 us (52%)
  waiting for transfers between devices  11.9 us (24%)
  Pallas kernels  10.1 us (20%)
  between operations  2.02 us (4%)
    ppermute x5, waiting for transfers between devices, shift_x(): return lax.ppermute(value, 'blk', pairs)  8.37 us
    ppermute x5, starting transfers between devices, shift_x(): return lax.ppermute(value, 'blk', pairs)  8.21 us
    ppermute x5, starting transfers between devices, shift_prev(): lax.ppermute(value, 'outer', [(s, (s + steps) % count) for s in range(cou...  8.05 us
    ppermute x2, starting transfers between devices, swap_z(): return lax.ppermute(value, 'blk', pairs)  8.02 us
    pallas_call x8, Pallas kernels, call(): pl.pallas_call(body, out_shape=outs, in_specs=specs, out_specs=[pl.BlockS...  8.01 us
    ppermute x5, waiting for transfers between devices, shift_prev(): lax.ppermute(value, 'outer', [(s, (s + steps) % count) for s in range(cou...  2.55 us
    pallas_call x2, Pallas kernels, finish(): pl.pallas_call(finish_kernel, out_shape=jax.ShapeDtypeStruct(raw.shape, B...  2.12 us
    ppermute x1, starting transfers between devices, shift_around(): return lax.ppermute(value, ('outer', 'blk'), pairs)  1.56 us
  transfers between devices with their start and end apart: 13, of which 8 were waited for; matrix products, arithmetic and copies ran while one was open for 0% of the time, Pallas kernels for 18%

profile of v4, /device:TPU:0, one launch (start us, length us, event | category | flops | bytes accessed | tf_op | source)
XLA Modules:
  0.0 49.9 jit_solution(8600872311329774811)
XLA Ops:
  0.6 1.6 %collective-permute-start = (bf16[160,1152]{1,0:T(8,128)(2,1)}, bf16[160,1152]{1,0:T(8,128)(2,1)S(1)}, u32[]{:S(2)}, u32[]{:S(2)}) collective-permute-start(bf16[160,1152]{1,0:T(8,128)(2,1)} %raw.2), channel_id=1, source_target_pairs={{0,2},{1,3},{2,4},{3,5},{4,6},{5,7},{6,0},{7,1},{8,10},{9,11},{10,... | collective-permute-start | bytes 1105928 | tf_op jit(solution)/shard_map/ppermute | solution.py:28
  2.3 1.7 %collective-permute-start.1 = (bf16[160,1152]{1,0:T(8,128)(2,1)}, bf16[160,1152]{1,0:T(8,128)(2,1)S(1)}, u32[]{:S(2)}, u32[]{:S(2)}) collective-permute-start(bf16[160,1152]{1,0:T(8,128)(2,1)} %raw.2), channel_id=1, source_target_pairs={{0,6},{1,7},{2,0},{3,1},{4,2},{5,3},{6,4},{7,5},{8,14},{9,15},{10,... | collective-permute-start | bytes 1105928 | tf_op jit(solution)/shard_map/ppermute | solution.py:28
  3.9 4.0 %collective-permute-start.3 = (bf16[160,1152]{1,0:T(8,128)(2,1)}, bf16[160,1152]{1,0:T(8,128)(2,1)S(1)}, u32[]{:S(2)}, u32[]{:S(2)}) collective-permute-start(bf16[160,1152]{1,0:T(8,128)(2,1)} %raw.3), channel_id=1, source_target_pairs={{0,1},{1,0},{2,3},{3,2},{4,5},{5,4},{6,7},{7,6},{8,9},{9,8},{10,11... | collective-permute-start | bytes 1105928 | tf_op jit(solution)/shard_map/ppermute | solution.py:47
  9.2 3.1 %collective-permute-done.x1_raw = bf16[160,1152]{1,0:T(8,128)(2,1)S(1)} collective-permute-done((bf16[160,1152]{1,0:T(8,128)(2,1)}, bf16[160,1152]{1,0:T(8,128)(2,1)S(1)}, u32[]{:S(2)}, u32[]{:S(2)}) %collective-permute-start) | collective-permute-done | bytes 368672 | tf_op jit(solution)/shard_map/ppermute | solution.py:28
  12.8 1.6 %collective-permute-start.2 = (bf16[160,1152]{1,0:T(8,128)(2,1)S(1)}, bf16[160,1152]{1,0:T(8,128)(2,1)S(1)}, u32[]{:S(2)}, u32[]{:S(2)}) collective-permute-start(bf16[160,1152]{1,0:T(8,128)(2,1)S(1)} %get-tuple-element.26), channel_id=1, source_target_pairs={{0,2},{1,3},{2,4},{3,5},{4,6},{5,7},{6,0},{7,1},{8,14},{9,15},{10,... | collective-permute-start | bytes 1105928 | tf_op jit(solution)/shard_map/ppermute | solution.py:38
  14.4 3.9 %collective-permute-start.7 = (bf16[320,1152]{1,0:T(8,128)(2,1)S(1)}, bf16[320,1152]{1,0:T(8,128)(2,1)S(1)}, u32[]{:S(2)}, u32[]{:S(2)}) collective-permute-start(bf16[320,1152]{1,0:T(8,128)(2,1)S(1)} %get-tuple-element.28.pair), channel_id=1, source_target_pairs={{0,120},{8,0},{16,8},{24,16},{32,24},{40,32},{48,40},{56,48},{64,5... | collective-permute-start | bytes 2211848 | tf_op jit(solution)/shard_map/ppermute | solution.py:19
  18.6 3.8 %collective-permute-start.6 = (bf16[160,1152]{1,0:T(8,128)(2,1)S(1)}, bf16[160,1152]{1,0:T(8,128)(2,1)S(1)}, u32[]{:S(2)}, u32[]{:S(2)}) collective-permute-start(bf16[160,1152]{1,0:T(8,128)(2,1)S(1)} %copy-done), channel_id=1, source_target_pairs={{0,120},{8,0},{16,8},{24,16},{32,24},{40,32},{48,40},{56,48},{64,5... | collective-permute-start | bytes 1105928 | tf_op jit(solution)/shard_map/ppermute | solution.py:19
  22.7 0.8 %collective-permute-done.4.p0_raw = bf16[160,1152]{1,0:T(8,128)(2,1)S(1)} collective-permute-done((bf16[160,1152]{1,0:T(8,128)(2,1)S(1)}, bf16[160,1152]{1,0:T(8,128)(2,1)S(1)}, u32[]{:S(2)}, u32[]{:S(2)}) %collective-permute-start.4) | collective-permute-done | bytes 368672 | tf_op jit(solution)/shard_map/ppermute | solution.py:19
  23.5 1.2 %early_pairs.1 = (bf16[640,1152]{1,0:T(8,128)(2,1)S(1)}, bf16[640,1152]{1,0:T(8,128)(2,1)S(1)}, bf16[640,640]{1,0:T(8,128)(2,1)S(1)}) custom-call(f32[1]{0:T(128)S(6)} %copy.14.temp, f32[1]{0:T(128)S(6)} %copy.15.bias, bf16[160,1152]{1,0:T(8,128)(2,1)S(1)} %copy-done, bf16[160,1152]{1,0:T(8,128)(2,1)S(1)} %copy-done.1, bf16[160,1152]{1,0:T(8,128)(2,1)S(1)} %unit_part.1.part, ...), custom_call_target="tpu_custom_call" | custom-call | flops 3000000000 | tf_op jit(solution)/shard_map/early_pairs/pallas_call | solution.py:53
  24.6 1.2 %far_pairs.1 = (bf16[640,1152]{1,0:T(8,128)(2,1)S(1)}, bf16[640,640]{1,0:T(8,128)(2,1)S(1)}, f32[480,1152]{1,0:T(8,128)S(1)}) custom-call(f32[1]{0:T(128)S(6)} %copy.14.temp, f32[1]{0:T(128)S(6)} %copy.15.bias, bf16[160,1152]{1,0:T(8,128)(2,1)S(1)} %collective-permute-done.2.x2, ...), custom_call_target="tpu_custom_call", output_to_operand_aliasing={{0}: (4, {}), {1}: (5, {})} | custom-call | flops 1000000000 | tf_op jit(solution)/shard_map/far_pairs/pallas_call | solution.py:53
  25.8 1.8 %collective-permute-done.5.p1 = bf16[160,1152]{1,0:T(8,128)(2,1)S(1)} collective-permute-done((bf16[160,1152]{1,0:T(8,128)(2,1)S(1)}, bf16[160,1152]{1,0:T(8,128)(2,1)S(1)}, u32[]{:S(2)}, u32[]{:S(2)}) %collective-permute-start.5) | collective-permute-done | bytes 368672 | tf_op jit(solution)/shard_map/ppermute | solution.py:19
  27.6 1.5 %late_pairs.1 = (bf16[640,1152]{1,0:T(8,128)(2,1)S(1)}, bf16[640,640]{1,0:T(8,128)(2,1)S(1)}, bf16[160,1152]{1,0:T(8,128)(2,1)S(1)}, bf16[160,1152]{1,0:T(8,128)(2,1)S(1)}, bf16[160,1152]{1,0:T(8,128)(2,1)S(1)}) custom-call(f32[1]{0:T(128)S(6)} %copy.14.temp, f32[1]{0:T(128)S(6)} %copy.15.bias, ...), custom_call_target="tpu_custom_call", output_to_operand_aliasing={{0}: (5, {}), {1}: (6, {})} | custom-call | flops 1000000000 | tf_op jit(solution)/shard_map/late_pairs/pallas_call | solution.py:53
  29.1 2.9 %collective-permute-start.10 = (bf16[160,1152]{1,0:T(8,128)(2,1)S(1)}, bf16[160,1152]{1,0:T(8,128)(2,1)S(1)}, u32[]{:S(2)}, u32[]{:S(2)}) collective-permute-start(bf16[160,1152]{1,0:T(8,128)(2,1)S(1)} %get-tuple-element.41), channel_id=1, source_target_pairs={{0,4},{1,5},{2,6},{3,7},{4,0},{5,1},{6,2},{7,3},{8,12},{9,13},{10,... | collective-permute-start | bytes 1105928 | tf_op jit(solution)/shard_map/ppermute | solution.py:28
  32.0 1.1 %collective-permute-start.8 = (bf16[160,1152]{1,0:T(8,128)(2,1)S(1)}, bf16[160,1152]{1,0:T(8,128)(2,1)S(1)}, u32[]{:S(2)}, u32[]{:S(2)}) collective-permute-start(bf16[160,1152]{1,0:T(8,128)(2,1)S(1)} %get-tuple-element.39), channel_id=1, source_target_pairs={{0,6},{1,7},{2,0},{3,1},{4,2},{5,3},{6,4},{7,5},{8,14},{9,15},{10,... | collective-permute-start | bytes 1105928 | tf_op jit(solution)/shard_map/ppermute | solution.py:28
  33.1 1.0 %collective-permute-start.9 = (bf16[160,1152]{1,0:T(8,128)(2,1)S(1)}, bf16[160,1152]{1,0:T(8,128)(2,1)S(1)}, u32[]{:S(2)}, u32[]{:S(2)}) collective-permute-start(bf16[160,1152]{1,0:T(8,128)(2,1)S(1)} %get-tuple-element.40), channel_id=1, source_target_pairs={{0,2},{1,3},{2,4},{3,5},{4,6},{5,7},{6,0},{7,1},{8,10},{9,11},{10,... | collective-permute-start | bytes 1105928 | tf_op jit(solution)/shard_map/ppermute | solution.py:28
  34.0 2.4 %middle_sums.1 = (f32[160,1152]{1,0:T(8,128)S(1)}, f32[160,1152]{1,0:T(8,128)S(1)}, f32[160,1152]{1,0:T(8,128)S(1)}) custom-call(f32[1]{0:T(128)S(6)} %copy.14.temp, f32[1]{0:T(128)S(6)} %copy.15.bias, bf16[640,1152]{1,0:T(8,128)(2,1)S(1)} %get-tuple-element.32.img, bf16[640,1152]{1,0:T(8,128)(2,1)S(1)} %get-tuple-element.35.txt, ...), custom_call_target="tpu_custom_call" | custom-call | flops 1000000000 | tf_op jit(solution)/shard_map/middle_sums/pallas_call | solution.py:53
  36.5 0.9 %part_sums.1 = (bf16[160,320]{1,0:T(8,128)(2,1)S(1)}, bf16[160,1152]{1,0:T(8,128)(2,1)S(1)}) custom-call(f32[1]{0:T(128)S(6)} %copy.14.temp, f32[1]{0:T(128)S(6)} %copy.15.bias, bf16[160,1152]{1,0:T(8,128)(2,1)S(1)} %collective-permute-done.11.n2, bf16[640,1152]{1,0:T(8,128)(2,1)S(1)} %get-tuple-element.35.txt, f32[160,1152]{1,0:T(8,128)S(1)} %get-tuple-element.43.e_part), custom_call_target="tpu_custom_call" | custom-call | flops 1000000000 | tf_op jit(solution)/shard_map/part_sums/pallas_call | solution.py:53
  37.4 4.1 %collective-permute-start.12 = (bf16[160,1152]{1,0:T(8,128)(2,1)S(1)}, bf16[160,1152]{1,0:T(8,128)(2,1)S(1)}, u32[]{:S(2)}, u32[]{:S(2)}) collective-permute-start(bf16[160,1152]{1,0:T(8,128)(2,1)S(1)} %get-tuple-element.45), channel_id=1, source_target_pairs={{0,1},{1,0},{2,3},{3,2},{4,5},{5,4},{6,7},{7,6},{8,9},{9,8},{10,11... | collective-permute-start | bytes 1105928 | tf_op jit(solution)/shard_map/ppermute | solution.py:47
  41.8 0.5 collective-permute-done.10.rest_2_
  42.2 3.9 %collective-permute-done.8.rest_0_ = bf16[160,1152]{1,0:T(8,128)(2,1)S(1)} collective-permute-done((bf16[160,1152]{1,0:T(8,128)(2,1)S(1)}, bf16[160,1152]{1,0:T(8,128)(2,1)S(1)}, u32[]{:S(2)}, u32[]{:S(2)}) %collective-permute-start.8) | collective-permute-done | bytes 368672 | tf_op jit(solution)/shard_map/ppermute | solution.py:28
  46.1 0.7 %collective-permute-done.9.rest_1_ = bf16[160,1152]{1,0:T(8,128)(2,1)S(1)} collective-permute-done((bf16[160,1152]{1,0:T(8,128)(2,1)S(1)}, bf16[160,1152]{1,0:T(8,128)(2,1)S(1)}, u32[]{:S(2)}, u32[]{:S(2)}) %collective-permute-start.9) | collective-permute-done | bytes 368672 | tf_op jit(solution)/shard_map/ppermute | solution.py:28
  46.8 1.1 %finish_images.1 = bf16[160,1152]{1,0:T(8,128)(2,1)} custom-call(bf16[160,1152]{1,0:T(8,128)(2,1)S(1)} %copy-done, f32[160,1152]{1,0:T(8,128)S(1)} %get-tuple-element.38.own, bf16[160,1152]{1,0:T(8,128)(2,1)S(1)} %collective-permute-done.8.rest_0_, bf16[160,1152]{1,0:T(8,128)(2,1)S(1)} %collective-permute-done.9.rest_1_, ...), custom_call_target="tpu_custom_call" | custom-call | flops 1000000000 | tf_op jit(solution)/shard_map/finish_images/pallas_call | solution.py:189
  47.9 0.9 %collective-permute-done.12.rest_0_ = bf16[160,1152]{1,0:T(8,128)(2,1)S(1)} collective-permute-done((bf16[160,1152]{1,0:T(8,128)(2,1)S(1)}, bf16[160,1152]{1,0:T(8,128)(2,1)S(1)}, u32[]{:S(2)}, u32[]{:S(2)}) %collective-permute-start.12) | collective-permute-done | bytes 368672 | tf_op jit(solution)/shard_map/ppermute | solution.py:47
  48.8 1.0 %finish_texts.1 = bf16[160,1152]{1,0:T(8,128)(2,1)} custom-call(bf16[160,1152]{1,0:T(8,128)(2,1)S(1)} %copy-done.1, f32[160,1152]{1,0:T(8,128)S(1)} %own_sums.1.own, bf16[160,1152]{1,0:T(8,128)(2,1)S(1)} %collective-permute-done.12.rest_0_), custom_call_target="tpu_custom_call" | custom-call | flops 1000000000 | tf_op jit(solution)/shard_map/finish_texts/pallas_call | solution.py:189
  (16 shorter events, 1.3 us)
Async XLA Ops:
  0.6 11.7 %collective-permute-start = (bf16[160,1152]{1,0:T(8,128)(2,1)}, bf16[160,1152]{1,0:T(8,128)(2,1)S(1)}, u32[]{:S(2)}, u32[]{:S(2)}) collective-permute-start(bf16[160,1152]{1,0:T(8,128)(2,1)} %raw.2), channel_id=1, source_target_pairs={{0,2},{1,3},{2,4},{3,5},{4,6},{5,7},{6,0},{7,1},{8,10},{9,11},{10,... | collective-permute-start | bytes 1105928 | tf_op jit(solution)/shard_map/ppermute | solution.py:28
  2.3 10.3 %collective-permute-start.1 = (bf16[160,1152]{1,0:T(8,128)(2,1)}, bf16[160,1152]{1,0:T(8,128)(2,1)S(1)}, u32[]{:S(2)}, u32[]{:S(2)}) collective-permute-start(bf16[160,1152]{1,0:T(8,128)(2,1)} %raw.2), channel_id=1, source_target_pairs={{0,6},{1,7},{2,0},{3,1},{4,2},{5,3},{6,4},{7,5},{8,14},{9,15},{10,... | collective-permute-start | bytes 1105928 | tf_op jit(solution)/shard_map/ppermute | solution.py:28
  3.9 14.3 %collective-permute-start.3 = (bf16[160,1152]{1,0:T(8,128)(2,1)}, bf16[160,1152]{1,0:T(8,128)(2,1)S(1)}, u32[]{:S(2)}, u32[]{:S(2)}) collective-permute-start(bf16[160,1152]{1,0:T(8,128)(2,1)} %raw.3), channel_id=1, source_target_pairs={{0,1},{1,0},{2,3},{3,2},{4,5},{5,4},{6,7},{7,6},{8,9},{9,8},{10,11... | collective-permute-start | bytes 1105928 | tf_op jit(solution)/shard_map/ppermute | solution.py:47
  12.5 1.9 %copy-start.1 = (bf16[160,1152]{1,0:T(8,128)(2,1)S(1)}, bf16[160,1152]{1,0:T(8,128)(2,1)}, u32[]{:S(2)}) copy-start(bf16[160,1152]{1,0:T(8,128)(2,1)} %raw.3) | copy-start | bytes 1105924
  12.8 9.5 %collective-permute-start.2 = (bf16[160,1152]{1,0:T(8,128)(2,1)S(1)}, bf16[160,1152]{1,0:T(8,128)(2,1)S(1)}, u32[]{:S(2)}, u32[]{:S(2)}) collective-permute-start(bf16[160,1152]{1,0:T(8,128)(2,1)S(1)} %get-tuple-element.26), channel_id=1, source_target_pairs={{0,2},{1,3},{2,4},{3,5},{4,6},{5,7},{6,0},{7,1},{8,14},{9,15},{10,... | collective-permute-start | bytes 1105928 | tf_op jit(solution)/shard_map/ppermute | solution.py:38
  14.4 9.0 %collective-permute-start.4 = (bf16[160,1152]{1,0:T(8,128)(2,1)S(1)}, bf16[160,1152]{1,0:T(8,128)(2,1)S(1)}, u32[]{:S(2)}, u32[]{:S(2)}) collective-permute-start(bf16[160,1152]{1,0:T(8,128)(2,1)S(1)} %copy-done.1), channel_id=1, source_target_pairs={{0,8},{8,16},{16,24},{24,32},{32,40},{40,48},{48,56},{56,64},{64,7... | collective-permute-start | bytes 1105928 | tf_op jit(solution)/shard_map/ppermute | solution.py:19
  14.4 4.1 %copy-start = (bf16[160,1152]{1,0:T(8,128)(2,1)S(1)}, bf16[160,1152]{1,0:T(8,128)(2,1)}, u32[]{:S(2)}) copy-start(bf16[160,1152]{1,0:T(8,128)(2,1)} %raw.2) | copy-start | bytes 1105924
  14.4 19.6 %collective-permute-start.7 = (bf16[320,1152]{1,0:T(8,128)(2,1)S(1)}, bf16[320,1152]{1,0:T(8,128)(2,1)S(1)}, u32[]{:S(2)}, u32[]{:S(2)}) collective-permute-start(bf16[320,1152]{1,0:T(8,128)(2,1)S(1)} %get-tuple-element.28.pair), channel_id=1, source_target_pairs={{0,120},{8,0},{16,8},{24,16},{32,24},{40,32},{48,40},{56,48},{64,5... | collective-permute-start | bytes 2211848 | tf_op jit(solution)/shard_map/ppermute | solution.py:19
  18.5 9.1 %collective-permute-start.5 = (bf16[160,1152]{1,0:T(8,128)(2,1)S(1)}, bf16[160,1152]{1,0:T(8,128)(2,1)S(1)}, u32[]{:S(2)}, u32[]{:S(2)}) collective-permute-start(bf16[160,1152]{1,0:T(8,128)(2,1)S(1)} %unit_part.1.part), channel_id=1, source_target_pairs={{0,8},{8,16},{16,24},{24,32},{32,40},{40,48},{48,56},{56,64},{64,7... | collective-permute-start | bytes 1105928 | tf_op jit(solution)/shard_map/ppermute | solution.py:19
  18.6 14.5 %collective-permute-start.6 = (bf16[160,1152]{1,0:T(8,128)(2,1)S(1)}, bf16[160,1152]{1,0:T(8,128)(2,1)S(1)}, u32[]{:S(2)}, u32[]{:S(2)}) collective-permute-start(bf16[160,1152]{1,0:T(8,128)(2,1)S(1)} %copy-done), channel_id=1, source_target_pairs={{0,120},{8,0},{16,8},{24,16},{32,24},{40,32},{48,40},{56,48},{64,5... | collective-permute-start | bytes 1105928 | tf_op jit(solution)/shard_map/ppermute | solution.py:19
  22.4 14.1 %collective-permute-start.11 = (bf16[160,1152]{1,0:T(8,128)(2,1)S(1)}, bf16[160,1152]{1,0:T(8,128)(2,1)S(1)}, u32[]{:S(2)}, u32[]{:S(2)}) collective-permute-start(bf16[160,1152]{1,0:T(8,128)(2,1)S(1)} %collective-permute-done.2.x2), channel_id=1, source_target_pairs={{0,120},{8,0},{16,8},{24,16},{32,24},{40,32},{48,40},{56,48},{64,5... | collective-permute-start | bytes 1105928 | tf_op jit(solution)/shard_map/ppermute | solution.py:19
  29.1 13.1 %collective-permute-start.10 = (bf16[160,1152]{1,0:T(8,128)(2,1)S(1)}, bf16[160,1152]{1,0:T(8,128)(2,1)S(1)}, u32[]{:S(2)}, u32[]{:S(2)}) collective-permute-start(bf16[160,1152]{1,0:T(8,128)(2,1)S(1)} %get-tuple-element.41), channel_id=1, source_target_pairs={{0,4},{1,5},{2,6},{3,7},{4,0},{5,1},{6,2},{7,3},{8,12},{9,13},{10,... | collective-permute-start | bytes 1105928 | tf_op jit(solution)/shard_map/ppermute | solution.py:28
  32.0 14.1 %collective-permute-start.8 = (bf16[160,1152]{1,0:T(8,128)(2,1)S(1)}, bf16[160,1152]{1,0:T(8,128)(2,1)S(1)}, u32[]{:S(2)}, u32[]{:S(2)}) collective-permute-start(bf16[160,1152]{1,0:T(8,128)(2,1)S(1)} %get-tuple-element.39), channel_id=1, source_target_pairs={{0,6},{1,7},{2,0},{3,1},{4,2},{5,3},{6,4},{7,5},{8,14},{9,15},{10,... | collective-permute-start | bytes 1105928 | tf_op jit(solution)/shard_map/ppermute | solution.py:28
  33.1 13.7 %collective-permute-start.9 = (bf16[160,1152]{1,0:T(8,128)(2,1)S(1)}, bf16[160,1152]{1,0:T(8,128)(2,1)S(1)}, u32[]{:S(2)}, u32[]{:S(2)}) collective-permute-start(bf16[160,1152]{1,0:T(8,128)(2,1)S(1)} %get-tuple-element.40), channel_id=1, source_target_pairs={{0,2},{1,3},{2,4},{3,5},{4,6},{5,7},{6,0},{7,1},{8,10},{9,11},{10,... | collective-permute-start | bytes 1105928 | tf_op jit(solution)/shard_map/ppermute | solution.py:28
  37.4 11.4 %collective-permute-start.12 = (bf16[160,1152]{1,0:T(8,128)(2,1)S(1)}, bf16[160,1152]{1,0:T(8,128)(2,1)S(1)}, u32[]{:S(2)}, u32[]{:S(2)}) collective-permute-start(bf16[160,1152]{1,0:T(8,128)(2,1)S(1)} %get-tuple-element.45), channel_id=1, source_target_pairs={{0,1},{1,0},{2,3},{3,2},{4,5},{5,4},{6,7},{7,6},{8,9},{9,8},{10,11... | collective-permute-start | bytes 1105928 | tf_op jit(solution)/shard_map/ppermute | solution.py:47

commit v5 on v4

--- a/solution.py
+++ b/solution.py
@@ -135,18 +135,15 @@
         out[...] = total[k * rows : (k + 1) * rows, :].astype(BF16)
 
 
-def middle_kernel(
-    temp, bias, img, txt, sig, n0_raw, n_pair, d0, e_own, e_part, nxt, sig_next
-):
-    rows = d0.shape[0]
-    d0[...] = temp[0] * jnp.dot(sig[:rows, :], txt[...], preferred_element_type=F32)
+def middle_kernel(temp, bias, img, txt, sig, n0_raw, n_pair, e_part, nxt, sig_near):
+    rows = n0_raw.shape[0]
     nxt[:rows, :] = normalized(n0_raw)
     nxt[rows:, :] = n_pair[...]
     value = scores(nxt[...], txt[: 2 * rows, :])
-    sig_next[...] = jax.nn.sigmoid(temp[0] * value + bias[0]).astype(BF16)
-    for k, out in enumerate((e_own, e_part)):
-        mine = slice(k * rows, (k + 1) * rows)
-        out[...] = temp[0] * (sums(sig[:, mine], img[...]) + sums(sig_next[:, mine], nxt[...]))
+    sig_near[...] = jax.nn.sigmoid(temp[0] * value + bias[0]).astype(BF16)
+    mine = slice(rows, 2 * rows)
+    total = sums(sig[:, mine], img[...]) + sums(sig_near[:, mine], nxt[...])
+    e_part[...] = temp[0] * total
 
 
 def part_kernel(temp, bias, n2, txt, e_part, sig_next, to_part):
@@ -157,9 +154,11 @@
     to_part[...] = total.astype(BF16)
 
 
-def own_kernel(temp, e_own, n2, sig_next, out):
-    rows = out.shape[0]
-    out[...] = e_own[...] + temp[0] * sums(sig_next[:, :rows], n2[...])
+def own_kernel(temp, img, txt, sig, nxt, sig_near, n2, sig_next, d0, e_own):
+    rows = d0.shape[0]
+    d0[...] = temp[0] * jnp.dot(sig[:rows, :], txt[...], preferred_element_type=F32)
+    total = sums(sig[:, :rows], img[...]) + sums(sig_near[:, :rows], nxt[...])
+    e_own[...] = temp[0] * (total + sums(sig_next[:, :rows], n2[...]))
 
 
 def finish_kernel(raw, own, *rest):
@@ -210,6 +209,8 @@
     halves = jax.ShapeDtypeStruct((rows, 2 * rows), BF16)
     wide = jax.ShapeDtypeStruct((2 * rows, width), BF16)
     triple = jax.ShapeDtypeStruct((3 * rows, width), F32)
+    triple_16 = jax.ShapeDtypeStruct((3 * rows, width), BF16)
+    thirds = jax.ShapeDtypeStruct((3 * rows, 2 * rows), BF16)
     core = (lax.axis_index("outer") % 2).astype(jnp.int32).reshape(1)
 
     part_raw = swap_z(texts)
@@ -243,18 +244,20 @@
     r1 = shift_x(d1, -1)
     r3 = shift_x(d3, 1)
     r2 = shift_x(d2, 2)
-    d0, e_own, e_part = call(
-        middle_kernel, "middle_sums", [f32] * 3, 1000000000,
-        (temp, bias, img, txt, sig, n0_raw, n_pair),
-        [VMEM((3 * rows, width), BF16), VMEM((3 * rows, 2 * rows), BF16)], smem=2,
+    e_part, nxt, sig_near = call(
+        middle_kernel, "middle_sums", [f32, triple_16, thirds], 1000000000,
+        (temp, bias, img, txt, sig, n0_raw, n_pair), smem=2,
     )
     sig_next, to_part = call(
         part_kernel, "part_sums", [halves, b16], 1000000000,
         (temp, bias, n2, txt, e_part), smem=2,
     )
     from_part = swap_z(to_part)
-    (e_own,) = call(own_kernel, "own_sums", [f32], 1000000000, (temp, e_own, n2, sig_next), smem=1)
-    grad_images = finish("finish_images", 1000000000, (images, d0, r1, r3, r2))
+    d0, e_own = call(
+        own_kernel, "own_sums", [f32] * 2, 1000000000,
+        (temp, img, txt, sig, nxt, sig_near, n2, sig_next), smem=1,
+    )
+    grad_images = finish("finish_images", 1000000000, (images, d0, r3, r2, r1))
     grad_texts = finish("finish_texts", 1000000000, (texts, e_own, from_part))
     return (grad_images, grad_texts)
 

time: 50 us -> 50 us (level)
  waiting for transfers between devices: 11.9 us -> 11.4 us
  transfers between devices with their start and end apart: 13 -> 13, of which waited for: 8 -> 7; matrix products, arithmetic and copies ran while one was open for 0% -> 0% of each run, Pallas kernels for 18% -> 19%
where the time goes in v5:
time: 50 us; the launch traced here: 49.8 us
  starting transfers between devices  25.9 us (52%)
  waiting for transfers between devices  11.4 us (23%)
  Pallas kernels  10.5 us (21%)
  between operations  2.02 us (4%)
    pallas_call x8, Pallas kernels, call(): pl.pallas_call(body, out_shape=outs, in_specs=specs, out_specs=[pl.BlockS...  8.43 us
    ppermute x5, starting transfers between devices, shift_x(): return lax.ppermute(value, 'blk', pairs)  8.21 us
    ppermute x5, starting transfers between devices, shift_prev(): lax.ppermute(value, 'outer', [(s, (s + steps) % count) for s in range(cou...  8.05 us
    ppermute x2, starting transfers between devices, swap_z(): return lax.ppermute(value, 'blk', pairs)  8.03 us
    ppermute x5, waiting for transfers between devices, shift_x(): return lax.ppermute(value, 'blk', pairs)  7.94 us
    ppermute x5, waiting for transfers between devices, shift_prev(): lax.ppermute(value, 'outer', [(s, (s + steps) % count) for s in range(cou...  2.55 us
    pallas_call x2, Pallas kernels, finish(): pl.pallas_call(finish_kernel, out_shape=jax.ShapeDtypeStruct(raw.shape, B...  2.08 us
    ppermute x1, starting transfers between devices, shift_around(): return lax.ppermute(value, ('outer', 'blk'), pairs)  1.56 us
  transfers between devices with their start and end apart: 13, of which 7 were waited for; matrix products, arithmetic and copies ran while one was open for 0% of the time, Pallas kernels for 19%

profile of v5, /device:TPU:0, one launch (start us, length us, event | category | flops | bytes accessed | tf_op | source)
XLA Modules:
  0.0 49.8 jit_solution(5266413125968850038)
XLA Ops:
  0.6 1.6 %collective-permute-start = (bf16[160,1152]{1,0:T(8,128)(2,1)}, bf16[160,1152]{1,0:T(8,128)(2,1)S(1)}, u32[]{:S(2)}, u32[]{:S(2)}) collective-permute-start(bf16[160,1152]{1,0:T(8,128)(2,1)} %raw.2), channel_id=1, source_target_pairs={{0,2},{1,3},{2,4},{3,5},{4,6},{5,7},{6,0},{7,1},{8,10},{9,11},{10,... | collective-permute-start | bytes 1105928 | tf_op jit(solution)/shard_map/ppermute | solution.py:28
  2.3 1.7 %collective-permute-start.1 = (bf16[160,1152]{1,0:T(8,128)(2,1)}, bf16[160,1152]{1,0:T(8,128)(2,1)S(1)}, u32[]{:S(2)}, u32[]{:S(2)}) collective-permute-start(bf16[160,1152]{1,0:T(8,128)(2,1)} %raw.2), channel_id=1, source_target_pairs={{0,6},{1,7},{2,0},{3,1},{4,2},{5,3},{6,4},{7,5},{8,14},{9,15},{10,... | collective-permute-start | bytes 1105928 | tf_op jit(solution)/shard_map/ppermute | solution.py:28
  3.9 4.0 %collective-permute-start.3 = (bf16[160,1152]{1,0:T(8,128)(2,1)}, bf16[160,1152]{1,0:T(8,128)(2,1)S(1)}, u32[]{:S(2)}, u32[]{:S(2)}) collective-permute-start(bf16[160,1152]{1,0:T(8,128)(2,1)} %raw.3), channel_id=1, source_target_pairs={{0,1},{1,0},{2,3},{3,2},{4,5},{5,4},{6,7},{7,6},{8,9},{9,8},{10,11... | collective-permute-start | bytes 1105928 | tf_op jit(solution)/shard_map/ppermute | solution.py:47
  9.2 3.1 %collective-permute-done.x1_raw = bf16[160,1152]{1,0:T(8,128)(2,1)S(1)} collective-permute-done((bf16[160,1152]{1,0:T(8,128)(2,1)}, bf16[160,1152]{1,0:T(8,128)(2,1)S(1)}, u32[]{:S(2)}, u32[]{:S(2)}) %collective-permute-start) | collective-permute-done | bytes 368672 | tf_op jit(solution)/shard_map/ppermute | solution.py:28
  12.8 1.6 %collective-permute-start.2 = (bf16[160,1152]{1,0:T(8,128)(2,1)S(1)}, bf16[160,1152]{1,0:T(8,128)(2,1)S(1)}, u32[]{:S(2)}, u32[]{:S(2)}) collective-permute-start(bf16[160,1152]{1,0:T(8,128)(2,1)S(1)} %get-tuple-element.28), channel_id=1, source_target_pairs={{0,2},{1,3},{2,4},{3,5},{4,6},{5,7},{6,0},{7,1},{8,14},{9,15},{10,... | collective-permute-start | bytes 1105928 | tf_op jit(solution)/shard_map/ppermute | solution.py:38
  14.4 3.9 %collective-permute-start.7 = (bf16[320,1152]{1,0:T(8,128)(2,1)S(1)}, bf16[320,1152]{1,0:T(8,128)(2,1)S(1)}, u32[]{:S(2)}, u32[]{:S(2)}) collective-permute-start(bf16[320,1152]{1,0:T(8,128)(2,1)S(1)} %get-tuple-element.30.pair), channel_id=1, source_target_pairs={{0,120},{8,0},{16,8},{24,16},{32,24},{40,32},{48,40},{56,48},{64,5... | collective-permute-start | bytes 2211848 | tf_op jit(solution)/shard_map/ppermute | solution.py:19
  18.6 3.8 %collective-permute-start.6 = (bf16[160,1152]{1,0:T(8,128)(2,1)S(1)}, bf16[160,1152]{1,0:T(8,128)(2,1)S(1)}, u32[]{:S(2)}, u32[]{:S(2)}) collective-permute-start(bf16[160,1152]{1,0:T(8,128)(2,1)S(1)} %copy-done), channel_id=1, source_target_pairs={{0,120},{8,0},{16,8},{24,16},{32,24},{40,32},{48,40},{56,48},{64,5... | collective-permute-start | bytes 1105928 | tf_op jit(solution)/shard_map/ppermute | solution.py:19
  22.7 0.8 %collective-permute-done.4.p0_raw = bf16[160,1152]{1,0:T(8,128)(2,1)S(1)} collective-permute-done((bf16[160,1152]{1,0:T(8,128)(2,1)S(1)}, bf16[160,1152]{1,0:T(8,128)(2,1)S(1)}, u32[]{:S(2)}, u32[]{:S(2)}) %collective-permute-start.4) | collective-permute-done | bytes 368672 | tf_op jit(solution)/shard_map/ppermute | solution.py:19
  23.5 1.2 %early_pairs.1 = (bf16[640,1152]{1,0:T(8,128)(2,1)S(1)}, bf16[640,1152]{1,0:T(8,128)(2,1)S(1)}, bf16[640,640]{1,0:T(8,128)(2,1)S(1)}) custom-call(f32[1]{0:T(128)S(6)} %copy.14.temp, f32[1]{0:T(128)S(6)} %copy.15.bias, bf16[160,1152]{1,0:T(8,128)(2,1)S(1)} %copy-done, bf16[160,1152]{1,0:T(8,128)(2,1)S(1)} %copy-done.1, bf16[160,1152]{1,0:T(8,128)(2,1)S(1)} %unit_part.1.part, ...), custom_call_target="tpu_custom_call" | custom-call | flops 3000000000 | tf_op jit(solution)/shard_map/early_pairs/pallas_call | solution.py:53
  24.6 1.2 %far_pairs.1 = (bf16[640,1152]{1,0:T(8,128)(2,1)S(1)}, bf16[640,640]{1,0:T(8,128)(2,1)S(1)}, f32[480,1152]{1,0:T(8,128)S(1)}) custom-call(f32[1]{0:T(128)S(6)} %copy.14.temp, f32[1]{0:T(128)S(6)} %copy.15.bias, bf16[160,1152]{1,0:T(8,128)(2,1)S(1)} %collective-permute-done.2.x2, ...), custom_call_target="tpu_custom_call", output_to_operand_aliasing={{0}: (4, {}), {1}: (5, {})} | custom-call | flops 1000000000 | tf_op jit(solution)/shard_map/far_pairs/pallas_call | solution.py:53
  25.8 1.8 %collective-permute-done.5.p1 = bf16[160,1152]{1,0:T(8,128)(2,1)S(1)} collective-permute-done((bf16[160,1152]{1,0:T(8,128)(2,1)S(1)}, bf16[160,1152]{1,0:T(8,128)(2,1)S(1)}, u32[]{:S(2)}, u32[]{:S(2)}) %collective-permute-start.5) | collective-permute-done | bytes 368672 | tf_op jit(solution)/shard_map/ppermute | solution.py:19
  27.6 1.5 %late_pairs.1 = (bf16[640,1152]{1,0:T(8,128)(2,1)S(1)}, bf16[640,640]{1,0:T(8,128)(2,1)S(1)}, bf16[160,1152]{1,0:T(8,128)(2,1)S(1)}, bf16[160,1152]{1,0:T(8,128)(2,1)S(1)}, bf16[160,1152]{1,0:T(8,128)(2,1)S(1)}) custom-call(f32[1]{0:T(128)S(6)} %copy.14.temp, f32[1]{0:T(128)S(6)} %copy.15.bias, ...), custom_call_target="tpu_custom_call", output_to_operand_aliasing={{0}: (5, {}), {1}: (6, {})} | custom-call | flops 1000000000 | tf_op jit(solution)/shard_map/late_pairs/pallas_call | solution.py:53
  29.1 2.9 %collective-permute-start.10 = (bf16[160,1152]{1,0:T(8,128)(2,1)S(1)}, bf16[160,1152]{1,0:T(8,128)(2,1)S(1)}, u32[]{:S(2)}, u32[]{:S(2)}) collective-permute-start(bf16[160,1152]{1,0:T(8,128)(2,1)S(1)} %get-tuple-element.46), channel_id=1, source_target_pairs={{0,4},{1,5},{2,6},{3,7},{4,0},{5,1},{6,2},{7,3},{8,12},{9,13},{10,... | collective-permute-start | bytes 1105928 | tf_op jit(solution)/shard_map/ppermute | solution.py:28
  32.0 1.1 %collective-permute-start.11 = (bf16[160,1152]{1,0:T(8,128)(2,1)S(1)}, bf16[160,1152]{1,0:T(8,128)(2,1)S(1)}, u32[]{:S(2)}, u32[]{:S(2)}) collective-permute-start(bf16[160,1152]{1,0:T(8,128)(2,1)S(1)} %get-tuple-element.47), channel_id=1, source_target_pairs={{0,6},{1,7},{2,0},{3,1},{4,2},{5,3},{6,4},{7,5},{8,14},{9,15},{10,... | collective-permute-start | bytes 1105928 | tf_op jit(solution)/shard_map/ppermute | solution.py:28
  33.1 1.0 %collective-permute-start.9 = (bf16[160,1152]{1,0:T(8,128)(2,1)S(1)}, bf16[160,1152]{1,0:T(8,128)(2,1)S(1)}, u32[]{:S(2)}, u32[]{:S(2)}) collective-permute-start(bf16[160,1152]{1,0:T(8,128)(2,1)S(1)} %get-tuple-element.45), channel_id=1, source_target_pairs={{0,2},{1,3},{2,4},{3,5},{4,6},{5,7},{6,0},{7,1},{8,10},{9,11},{10,... | collective-permute-start | bytes 1105928 | tf_op jit(solution)/shard_map/ppermute | solution.py:28
  34.0 2.0 %middle_sums.1 = (f32[160,1152]{1,0:T(8,128)S(1)}, bf16[480,1152]{1,0:T(8,128)(2,1)S(1)}, bf16[480,320]{1,0:T(8,128)(2,1)S(1)}) custom-call(f32[1]{0:T(128)S(6)} %copy.14.temp, f32[1]{0:T(128)S(6)} %copy.15.bias, bf16[640,1152]{1,0:T(8,128)(2,1)S(1)} %get-tuple-element.34.img, bf16[640,1152]{1,0:T(8,128)(2,1)S(1)} %get-tuple-element.37.txt, ...), custom_call_target="tpu_custom_call" | custom-call | flops 1000000000 | tf_op jit(solution)/shard_map/middle_sums/pallas_call | solution.py:53
  36.1 0.9 %part_sums.1 = (bf16[160,320]{1,0:T(8,128)(2,1)S(1)}, bf16[160,1152]{1,0:T(8,128)(2,1)S(1)}) custom-call(f32[1]{0:T(128)S(6)} %copy.14.temp, f32[1]{0:T(128)S(6)} %copy.15.bias, bf16[160,1152]{1,0:T(8,128)(2,1)S(1)} %collective-permute-done.8.n2, bf16[640,1152]{1,0:T(8,128)(2,1)S(1)} %get-tuple-element.37.txt, f32[160,1152]{1,0:T(8,128)S(1)} %get-tuple-element.42.e_part), custom_call_target="tpu_custom_call" | custom-call | flops 1000000000 | tf_op jit(solution)/shard_map/part_sums/pallas_call | solution.py:53
  37.0 4.1 %collective-permute-start.12 = (bf16[160,1152]{1,0:T(8,128)(2,1)S(1)}, bf16[160,1152]{1,0:T(8,128)(2,1)S(1)}, u32[]{:S(2)}, u32[]{:S(2)}) collective-permute-start(bf16[160,1152]{1,0:T(8,128)(2,1)S(1)} %get-tuple-element.49), channel_id=1, source_target_pairs={{0,1},{1,0},{2,3},{3,2},{4,5},{5,4},{6,7},{7,6},{8,9},{9,8},{10,11... | collective-permute-start | bytes 1105928 | tf_op jit(solution)/shard_map/ppermute | solution.py:47
  41.1 1.1 %own_sums.1 = (f32[160,1152]{1,0:T(8,128)S(1)}, f32[160,1152]{1,0:T(8,128)S(1)}) custom-call(f32[1]{0:T(128)S(6)} %copy.14.temp, bf16[640,1152]{1,0:T(8,128)(2,1)S(1)} %get-tuple-element.34.img, bf16[640,1152]{1,0:T(8,128)(2,1)S(1)} %get-tuple-element.37.txt, bf16[640,640]{1,0:T(8,128)(2,1)S(1)} %get-tuple-element.38.sig, ...), custom_call_target="tpu_custom_call" | custom-call | flops 1000000000 | tf_op jit(solution)/shard_map/own_sums/pallas_call | solution.py:53
  42.2 3.9 %collective-permute-done.11.rest_2_ = bf16[160,1152]{1,0:T(8,128)(2,1)S(1)} collective-permute-done((bf16[160,1152]{1,0:T(8,128)(2,1)S(1)}, bf16[160,1152]{1,0:T(8,128)(2,1)S(1)}, u32[]{:S(2)}, u32[]{:S(2)}) %collective-permute-start.11) | collective-permute-done | bytes 368672 | tf_op jit(solution)/shard_map/ppermute | solution.py:28
  46.1 0.7 %collective-permute-done.9.rest_0_ = bf16[160,1152]{1,0:T(8,128)(2,1)S(1)} collective-permute-done((bf16[160,1152]{1,0:T(8,128)(2,1)S(1)}, bf16[160,1152]{1,0:T(8,128)(2,1)S(1)}, u32[]{:S(2)}, u32[]{:S(2)}) %collective-permute-start.9) | collective-permute-done | bytes 368672 | tf_op jit(solution)/shard_map/ppermute | solution.py:28
  46.8 1.1 %finish_images.1 = bf16[160,1152]{1,0:T(8,128)(2,1)} custom-call(bf16[160,1152]{1,0:T(8,128)(2,1)S(1)} %copy-done, f32[160,1152]{1,0:T(8,128)S(1)} %get-tuple-element.44.own, bf16[160,1152]{1,0:T(8,128)(2,1)S(1)} %collective-permute-done.9.rest_0_, bf16[160,1152]{1,0:T(8,128)(2,1)S(1)} %collective-permute-done.10.rest_1_, ...), custom_call_target="tpu_custom_call" | custom-call | flops 1000000000 | tf_op jit(solution)/shard_map/finish_images/pallas_call | solution.py:188
  47.9 0.9 %collective-permute-done.12.rest_0_ = bf16[160,1152]{1,0:T(8,128)(2,1)S(1)} collective-permute-done((bf16[160,1152]{1,0:T(8,128)(2,1)S(1)}, bf16[160,1152]{1,0:T(8,128)(2,1)S(1)}, u32[]{:S(2)}, u32[]{:S(2)}) %collective-permute-start.12) | collective-permute-done | bytes 368672 | tf_op jit(solution)/shard_map/ppermute | solution.py:47
  48.8 1.0 %finish_texts.1 = bf16[160,1152]{1,0:T(8,128)(2,1)} custom-call(bf16[160,1152]{1,0:T(8,128)(2,1)S(1)} %copy-done.1, f32[160,1152]{1,0:T(8,128)S(1)} %get-tuple-element.48.own, bf16[160,1152]{1,0:T(8,128)(2,1)S(1)} %collective-permute-done.12.rest_0_), custom_call_target="tpu_custom_call" | custom-call | flops 1000000000 | tf_op jit(solution)/shard_map/finish_texts/pallas_call | solution.py:188
  (16 shorter events, 1.1 us)
Async XLA Ops:
  0.6 11.7 %collective-permute-start = (bf16[160,1152]{1,0:T(8,128)(2,1)}, bf16[160,1152]{1,0:T(8,128)(2,1)S(1)}, u32[]{:S(2)}, u32[]{:S(2)}) collective-permute-start(bf16[160,1152]{1,0:T(8,128)(2,1)} %raw.2), channel_id=1, source_target_pairs={{0,2},{1,3},{2,4},{3,5},{4,6},{5,7},{6,0},{7,1},{8,10},{9,11},{10,... | collective-permute-start | bytes 1105928 | tf_op jit(solution)/shard_map/ppermute | solution.py:28
  2.3 10.3 %collective-permute-start.1 = (bf16[160,1152]{1,0:T(8,128)(2,1)}, bf16[160,1152]{1,0:T(8,128)(2,1)S(1)}, u32[]{:S(2)}, u32[]{:S(2)}) collective-permute-start(bf16[160,1152]{1,0:T(8,128)(2,1)} %raw.2), channel_id=1, source_target_pairs={{0,6},{1,7},{2,0},{3,1},{4,2},{5,3},{6,4},{7,5},{8,14},{9,15},{10,... | collective-permute-start | bytes 1105928 | tf_op jit(solution)/shard_map/ppermute | solution.py:28
  3.9 14.3 %collective-permute-start.3 = (bf16[160,1152]{1,0:T(8,128)(2,1)}, bf16[160,1152]{1,0:T(8,128)(2,1)S(1)}, u32[]{:S(2)}, u32[]{:S(2)}) collective-permute-start(bf16[160,1152]{1,0:T(8,128)(2,1)} %raw.3), channel_id=1, source_target_pairs={{0,1},{1,0},{2,3},{3,2},{4,5},{5,4},{6,7},{7,6},{8,9},{9,8},{10,11... | collective-permute-start | bytes 1105928 | tf_op jit(solution)/shard_map/ppermute | solution.py:47
  12.5 1.9 %copy-start.1 = (bf16[160,1152]{1,0:T(8,128)(2,1)S(1)}, bf16[160,1152]{1,0:T(8,128)(2,1)}, u32[]{:S(2)}) copy-start(bf16[160,1152]{1,0:T(8,128)(2,1)} %raw.3) | copy-start | bytes 1105924
  12.8 9.5 %collective-permute-start.2 = (bf16[160,1152]{1,0:T(8,128)(2,1)S(1)}, bf16[160,1152]{1,0:T(8,128)(2,1)S(1)}, u32[]{:S(2)}, u32[]{:S(2)}) collective-permute-start(bf16[160,1152]{1,0:T(8,128)(2,1)S(1)} %get-tuple-element.28), channel_id=1, source_target_pairs={{0,2},{1,3},{2,4},{3,5},{4,6},{5,7},{6,0},{7,1},{8,14},{9,15},{10,... | collective-permute-start | bytes 1105928 | tf_op jit(solution)/shard_map/ppermute | solution.py:38
  14.4 9.0 %collective-permute-start.4 = (bf16[160,1152]{1,0:T(8,128)(2,1)S(1)}, bf16[160,1152]{1,0:T(8,128)(2,1)S(1)}, u32[]{:S(2)}, u32[]{:S(2)}) collective-permute-start(bf16[160,1152]{1,0:T(8,128)(2,1)S(1)} %copy-done.1), channel_id=1, source_target_pairs={{0,8},{8,16},{16,24},{24,32},{32,40},{40,48},{48,56},{56,64},{64,7... | collective-permute-start | bytes 1105928 | tf_op jit(solution)/shard_map/ppermute | solution.py:19
  14.4 4.1 %copy-start = (bf16[160,1152]{1,0:T(8,128)(2,1)S(1)}, bf16[160,1152]{1,0:T(8,128)(2,1)}, u32[]{:S(2)}) copy-start(bf16[160,1152]{1,0:T(8,128)(2,1)} %raw.2) | copy-start | bytes 1105924
  14.4 19.6 %collective-permute-start.7 = (bf16[320,1152]{1,0:T(8,128)(2,1)S(1)}, bf16[320,1152]{1,0:T(8,128)(2,1)S(1)}, u32[]{:S(2)}, u32[]{:S(2)}) collective-permute-start(bf16[320,1152]{1,0:T(8,128)(2,1)S(1)} %get-tuple-element.30.pair), channel_id=1, source_target_pairs={{0,120},{8,0},{16,8},{24,16},{32,24},{40,32},{48,40},{56,48},{64,5... | collective-permute-start | bytes 2211848 | tf_op jit(solution)/shard_map/ppermute | solution.py:19
  18.5 9.1 %collective-permute-start.5 = (bf16[160,1152]{1,0:T(8,128)(2,1)S(1)}, bf16[160,1152]{1,0:T(8,128)(2,1)S(1)}, u32[]{:S(2)}, u32[]{:S(2)}) collective-permute-start(bf16[160,1152]{1,0:T(8,128)(2,1)S(1)} %unit_part.1.part), channel_id=1, source_target_pairs={{0,8},{8,16},{16,24},{24,32},{32,40},{40,48},{48,56},{56,64},{64,7... | collective-permute-start | bytes 1105928 | tf_op jit(solution)/shard_map/ppermute | solution.py:19
  18.6 14.5 %collective-permute-start.6 = (bf16[160,1152]{1,0:T(8,128)(2,1)S(1)}, bf16[160,1152]{1,0:T(8,128)(2,1)S(1)}, u32[]{:S(2)}, u32[]{:S(2)}) collective-permute-start(bf16[160,1152]{1,0:T(8,128)(2,1)S(1)} %copy-done), channel_id=1, source_target_pairs={{0,120},{8,0},{16,8},{24,16},{32,24},{40,32},{48,40},{56,48},{64,5... | collective-permute-start | bytes 1105928 | tf_op jit(solution)/shard_map/ppermute | solution.py:19
  22.4 13.7 %collective-permute-start.8 = (bf16[160,1152]{1,0:T(8,128)(2,1)S(1)}, bf16[160,1152]{1,0:T(8,128)(2,1)S(1)}, u32[]{:S(2)}, u32[]{:S(2)}) collective-permute-start(bf16[160,1152]{1,0:T(8,128)(2,1)S(1)} %collective-permute-done.2.x2), channel_id=1, source_target_pairs={{0,120},{8,0},{16,8},{24,16},{32,24},{40,32},{48,40},{56,48},{64,5... | collective-permute-start | bytes 1105928 | tf_op jit(solution)/shard_map/ppermute | solution.py:19
  29.1 13.1 %collective-permute-start.10 = (bf16[160,1152]{1,0:T(8,128)(2,1)S(1)}, bf16[160,1152]{1,0:T(8,128)(2,1)S(1)}, u32[]{:S(2)}, u32[]{:S(2)}) collective-permute-start(bf16[160,1152]{1,0:T(8,128)(2,1)S(1)} %get-tuple-element.46), channel_id=1, source_target_pairs={{0,4},{1,5},{2,6},{3,7},{4,0},{5,1},{6,2},{7,3},{8,12},{9,13},{10,... | collective-permute-start | bytes 1105928 | tf_op jit(solution)/shard_map/ppermute | solution.py:28
  32.0 14.1 %collective-permute-start.11 = (bf16[160,1152]{1,0:T(8,128)(2,1)S(1)}, bf16[160,1152]{1,0:T(8,128)(2,1)S(1)}, u32[]{:S(2)}, u32[]{:S(2)}) collective-permute-start(bf16[160,1152]{1,0:T(8,128)(2,1)S(1)} %get-tuple-element.47), channel_id=1, source_target_pairs={{0,6},{1,7},{2,0},{3,1},{4,2},{5,3},{6,4},{7,5},{8,14},{9,15},{10,... | collective-permute-start | bytes 1105928 | tf_op jit(solution)/shard_map/ppermute | solution.py:28
  33.1 13.7 %collective-permute-start.9 = (bf16[160,1152]{1,0:T(8,128)(2,1)S(1)}, bf16[160,1152]{1,0:T(8,128)(2,1)S(1)}, u32[]{:S(2)}, u32[]{:S(2)}) collective-permute-start(bf16[160,1152]{1,0:T(8,128)(2,1)S(1)} %get-tuple-element.45), channel_id=1, source_target_pairs={{0,2},{1,3},{2,4},{3,5},{4,6},{5,7},{6,0},{7,1},{8,10},{9,11},{10,... | collective-permute-start | bytes 1105928 | tf_op jit(solution)/shard_map/ppermute | solution.py:28
  37.0 11.8 %collective-permute-start.12 = (bf16[160,1152]{1,0:T(8,128)(2,1)S(1)}, bf16[160,1152]{1,0:T(8,128)(2,1)S(1)}, u32[]{:S(2)}, u32[]{:S(2)}) collective-permute-start(bf16[160,1152]{1,0:T(8,128)(2,1)S(1)} %get-tuple-element.49), channel_id=1, source_target_pairs={{0,1},{1,0},{2,3},{3,2},{4,5},{5,4},{6,7},{7,6},{8,9},{9,8},{10,11... | collective-permute-start | bytes 1105928 | tf_op jit(solution)/shard_map/ppermute | solution.py:47
